TPU v7x, 32 devices: a whole 2x2x4 slice. The times are simulated.
32 devices in a mesh: seq: 8 (over z, x), head: 4 (over y, core).
Axes of the slice: x: 2, y: 2, z: 4, core: 2. Of those that a mesh axis runs over, the one named last changes fastest.
Arguments:
- tokens: bfloat16 [2, 2048, 768], P(None, ('seq', 'head')), may hold values from -6 to 6
- positions: int32 [2, 2048], P(None, 'seq'), may hold values from 0 to 2047, each once within a row
- w_qkv: bfloat16 [768, 2304], P(('seq', 'head')), may hold values from -0.21875 to 0.21875
- qv_bias: bfloat16 [2, 768], P(None, ('seq', 'head')), may hold values from -3 to 3
- w_attn_out: bfloat16 [768, 768], P(('seq', 'head')), may hold values from -0.875 to 0.875
- attn_out_bias: bfloat16 [768], P(('seq', 'head')), may hold values from -3 to 3
- norm1_gain: bfloat16 [768], P(('seq', 'head')), may hold values from 0.5 to 1.5
- norm1_bias: bfloat16 [768], P(('seq', 'head')), may hold values from -3 to 3
- w_in: bfloat16 [768, 6144], P(('seq', 'head')), may hold values from -0.21875 to 0.21875
- in_bias: bfloat16 [6144], P(('seq', 'head')), may hold values from -3 to 3
- w_out: bfloat16 [3072, 768], P(('seq', 'head')), may hold values from -0.109375 to 0.109375
- out_bias: bfloat16 [768], P(('seq', 'head')), may hold values from -3 to 3
- norm2_gain: bfloat16 [768], P(('seq', 'head')), may hold values from 0.5 to 1.5
- norm2_bias: bfloat16 [768], P(('seq', 'head')), may hold values from -3 to 3
- cotangent: bfloat16 [2, 2048, 768], P(None, ('seq', 'head')), may hold values from -6 to 6
Outputs:
- output: bfloat16 [2, 2048, 768], P(None, ('seq', 'head'))
- input_grad: float32 [2, 2048, 768], P(None, ('seq', 'head'))
- grad_w_qkv: float32 [768, 2304], P(('seq', 'head'))
- grad_qv_bias: float32 [2, 768], P(None, ('seq', 'head'))
- grad_w_attn_out: float32 [768, 768], P(('seq', 'head'))
- grad_attn_out_bias: float32 [768], P(('seq', 'head'))
- grad_norm1_gain: float32 [768], P(('seq', 'head'))
- grad_norm1_bias: float32 [768], P(('seq', 'head'))
- grad_w_in: float32 [768, 6144], P(('seq', 'head'))
- grad_in_bias: float32 [6144], P(('seq', 'head'))
- grad_w_out: float32 [3072, 768], P(('seq', 'head'))
- grad_out_bias: float32 [768], P(('seq', 'head'))
- grad_norm2_gain: float32 [768], P(('seq', 'head'))
- grad_norm2_bias: float32 [768], P(('seq', 'head'))
Inputs may be any that keep to these rules, and one draw needn't show every extreme that they name: `positions`: each row holds every position 0 to 2047 exactly once.
All inputs are finite; a program needn't handle non-finite values.
Results may differ from a plain program's by a relative error of at most 0.039.
Values may be sent and summed in bfloat16 or wider, within the bound.
No kernel may reach another device: no remote copies, remote signals or barrier semaphores. Data moves between devices by JAX's collectives and lax.ppermute only.
A program may use at most 192 MiB of HBM per device.

v0:
```python
import jax
import jax.numpy as jnp
from jax import lax
from jax.sharding import PartitionSpec as P

HEADS = 12
HEAD_DIM = 64


EPSILON = 1e-12
SCORE_SCALE = 0.125
LOWEST = -1e30


def layer_norm(values, gain_vec, offsets):
    average = jnp.mean(values, axis=-1, keepdims=True)
    centred = values - average
    variance = jnp.mean(centred * centred, axis=-1, keepdims=True)
    return centred * lax.rsqrt(variance + EPSILON) * gain_vec + offsets


def geglu(merged_heads):
    half_width = merged_heads.shape[-1] // 2
    return (
        jax.nn.gelu(merged_heads[..., :half_width], approximate=False)
        * merged_heads[..., half_width:]
    )


def alibi_scores(query_heads, key_heads, query_pos, key_pos, slopes):
    products = jnp.einsum(
        "shdq,shdk->shqk", query_heads, key_heads, preferred_element_type=jnp.float32
    )
    distances = jnp.abs(query_pos[:, :, None] - key_pos[:, None, :]).astype(jnp.float32)
    return products * SCORE_SCALE - slopes[None, :, None, None] * distances[:, None, :, :]


def score_terms(
    query_heads, out_grads, log_sum, deltas, query_pos, key_heads, value_heads, key_pos, slopes
):
    scores = alibi_scores(query_heads, key_heads, query_pos, key_pos, slopes)
    probabilities = jnp.exp(scores - log_sum[..., None])
    prob_grads = jnp.einsum(
        "shdq,shdk->shqk", out_grads, value_heads, preferred_element_type=jnp.float32
    )
    score_grads = (probabilities * (prob_grads - deltas[..., None])).astype(jnp.bfloat16)
    return (probabilities.astype(jnp.bfloat16), score_grads)


def over_blocks(advance, running, length, stride):

    def visit(number, current):
        return advance(current, number * stride, stride)

    return lax.fori_loop(0, length // stride, visit, running)


def split_pairs(stacked, head_count):
    seq_count = stacked.shape[0]
    length = stacked.shape[-1]
    paired = stacked.reshape(seq_count, 2, head_count, stacked.shape[1] // (2 * head_count), length)
    return (paired[:, 0], paired[:, 1])


def slice_last(array, offset, extent):
    return lax.dynamic_slice_in_dim(array, offset, extent, array.ndim - 1)


def body(
    tokens,
    positions,
    w_qkv,
    qv_bias,
    w_attn_out,
    attn_out_bias,
    norm1_gain,
    norm1_bias,
    w_in,
    in_bias,
    w_out,
    out_bias,
    norm2_gain,
    norm2_bias,
    cotangent,
):
    groups = lax.axis_size("head")
    seq_count, row_count, model_width = tokens.shape
    group_rows = positions.shape[1]
    head_count = HEADS // groups
    qkv_full, qv_full, attn_full, attn_bias_full, first_gain, first_offset = (
        lax.all_gather(w_qkv, ("seq", "head"), axis=0, tiled=True),
        lax.all_gather(qv_bias, ("seq", "head"), axis=1, tiled=True),
        lax.all_gather(w_attn_out, ("seq", "head"), axis=0, tiled=True),
        lax.all_gather(attn_out_bias, ("seq", "head"), axis=0, tiled=True),
        lax.all_gather(norm1_gain, ("seq", "head"), axis=0, tiled=True),
        lax.all_gather(norm1_bias, ("seq", "head"), axis=0, tiled=True),
    )
    inner_width = attn_full.shape[0]
    group_width = inner_width // groups
    head_ids = lax.axis_index("head") * head_count + jnp.arange(head_count)
    slopes = 2.0 ** (-8.0 * (head_ids + 1).astype(jnp.float32) / HEADS)
    column_bias_terms = jnp.concatenate(
        [qv_full[0], jnp.zeros((inner_width,), jnp.bfloat16), qv_full[1]]
    ).astype(jnp.float32)
    projection_result = (
        jnp.einsum("std,dc->sct", tokens, qkv_full, preferred_element_type=jnp.float32)
        + column_bias_terms[None, :, None]
    )
    outgoing = projection_result.astype(jnp.bfloat16).reshape(
        seq_count, 3, groups, group_width, row_count
    )
    arrived = lax.all_to_all(outgoing, "head", split_axis=2, concat_axis=4, tiled=True)
    query_heads = arrived[:, 0, 0].reshape(seq_count, head_count, HEAD_DIM, group_rows)
    key_values = arrived[:, 1:, 0].reshape(seq_count, 2 * group_width, group_rows)
    key_pos = positions.reshape(seq_count, 1, group_rows)
    own_keys, own_values = split_pairs(key_values, head_count)
    initial = (
        jnp.full((seq_count, head_count, group_rows), LOWEST, jnp.float32),
        jnp.zeros((seq_count, head_count, group_rows), jnp.float32),
        jnp.zeros((seq_count, head_count, HEAD_DIM, group_rows), jnp.float32),
    )
    block_kv = lax.all_gather(key_values, "seq", axis=2, tiled=True)
    block_pos = lax.all_gather(key_pos, "seq", axis=2, tiled=True)
    key_heads, value_heads = split_pairs(block_kv, head_count)

    def advance(current, offset, extent):
        row_max, row_sum, accumulated = current
        key_part = slice_last(key_heads, offset, extent)
        value_part = slice_last(value_heads, offset, extent)
        pos_part = slice_last(block_pos[:, 0], offset, extent)
        scores = alibi_scores(query_heads, key_part, positions, pos_part, slopes)
        new_max = jnp.maximum(row_max, jnp.max(scores, axis=-1))
        factor = jnp.exp(row_max - new_max)
        weights = jnp.exp(scores - new_max[..., None])
        row_sum = row_sum * factor + jnp.sum(weights, axis=-1)
        accumulated = accumulated * factor[:, :, None, :] + jnp.einsum(
            "shqk,shdk->shdq",
            weights.astype(jnp.bfloat16),
            value_part,
            preferred_element_type=jnp.float32,
        )
        return (new_max, row_sum, accumulated)

    row_max, row_sum, accumulated = over_blocks(advance, initial, block_kv.shape[2], group_rows)
    log_sum = row_max + jnp.log(row_sum)
    attention_result = accumulated / row_sum[:, :, None, :]
    attended_low = attention_result.astype(jnp.bfloat16).reshape(
        seq_count, 1, group_width, group_rows
    )
    returned = lax.all_to_all(attended_low, "head", split_axis=3, concat_axis=1, tiled=True)
    mixed_heads = returned.reshape(seq_count, inner_width, row_count)
    attention_linear = jnp.einsum(
        "sct,cd->std", mixed_heads, attn_full, preferred_element_type=jnp.float32
    ) + attn_bias_full.astype(jnp.float32)
    input_rows = tokens.astype(jnp.float32)
    hidden, first_back = jax.vjp(
        layer_norm,
        input_rows + attention_linear,
        first_gain.astype(jnp.float32),
        first_offset.astype(jnp.float32),
    )
    in_full, in_bias_full, out_full, out_bias_full, second_gain, second_offset = (
        lax.all_gather(w_in, ("seq", "head"), axis=0, tiled=True),
        lax.all_gather(in_bias, ("seq", "head"), axis=0, tiled=True),
        lax.all_gather(w_out, ("seq", "head"), axis=0, tiled=True),
        lax.all_gather(out_bias, ("seq", "head"), axis=0, tiled=True),
        lax.all_gather(norm2_gain, ("seq", "head"), axis=0, tiled=True),
        lax.all_gather(norm2_bias, ("seq", "head"), axis=0, tiled=True),
    )
    hidden_reduced = hidden.astype(jnp.bfloat16)
    merged_heads = jnp.einsum(
        "std,df->stf", hidden_reduced, in_full, preferred_element_type=jnp.float32
    ) + in_bias_full.astype(jnp.float32)
    gelu_activations, gate_back = jax.vjp(geglu, merged_heads)
    activated_low = gelu_activations.astype(jnp.bfloat16)
    feedforward_linear = jnp.einsum(
        "stf,fd->std", activated_low, out_full, preferred_element_type=jnp.float32
    ) + out_bias_full.astype(jnp.float32)
    result, second_back = jax.vjp(
        layer_norm,
        hidden + feedforward_linear,
        second_gain.astype(jnp.float32),
        second_offset.astype(jnp.float32),
    )
    second_grad, grad_gain_two, grad_offset_two = second_back(cotangent.astype(jnp.float32))
    ff_grad = second_grad.astype(jnp.bfloat16)
    grad_out_bias = jnp.sum(ff_grad.astype(jnp.float32), axis=(0, 1))
    grad_w_out = jnp.einsum(
        "stf,std->fd", activated_low, ff_grad, preferred_element_type=jnp.float32
    )
    act_grad = jnp.einsum("std,fd->stf", ff_grad, out_full, preferred_element_type=jnp.float32)
    joined_grad = gate_back(act_grad)[0].astype(jnp.bfloat16)
    grad_in_bias = jnp.sum(joined_grad.astype(jnp.float32), axis=(0, 1))
    grad_w_in = jnp.einsum(
        "std,stf->df", hidden_reduced, joined_grad, preferred_element_type=jnp.float32
    )
    hidden_grad = second_grad + jnp.einsum(
        "stf,df->std", joined_grad, in_full, preferred_element_type=jnp.float32
    )
    first_grad, grad_gain_one, grad_offset_one = first_back(hidden_grad)
    attn_grad = first_grad.astype(jnp.bfloat16)
    grad_attn_bias = jnp.sum(attn_grad.astype(jnp.float32), axis=(0, 1))
    grad_w_attn = jnp.einsum(
        "sct,std->cd", mixed_heads, attn_grad, preferred_element_type=jnp.float32
    )
    out_tokens = jnp.einsum(
        "std,cd->sct", attn_grad, attn_full, preferred_element_type=jnp.float32
    ).astype(jnp.bfloat16)
    out_arrived = lax.all_to_all(
        out_tokens.reshape(seq_count, groups, group_width, row_count),
        "head",
        split_axis=1,
        concat_axis=3,
        tiled=True,
    )
    out_grads = out_arrived.reshape(seq_count, head_count, HEAD_DIM, group_rows)
    deltas = jnp.sum(out_grads.astype(jnp.float32) * attention_result, axis=2)
    block_kv = lax.all_gather(key_values, "seq", axis=2, tiled=True)
    fold_block_pos = lax.all_gather(key_pos, "seq", axis=2, tiled=True)
    fold_key_heads, fold_value_heads = split_pairs(block_kv, head_count)

    def advance(current, offset, extent):
        key_part = slice_last(fold_key_heads, offset, extent)
        value_part = slice_last(fold_value_heads, offset, extent)
        pos_part = slice_last(fold_block_pos[:, 0], offset, extent)
        weights, score_grads = score_terms(
            query_heads,
            out_grads,
            log_sum,
            deltas,
            positions,
            key_part,
            value_part,
            pos_part,
            slopes,
        )
        return current + SCORE_SCALE * jnp.einsum(
            "shqk,shdk->shdq", score_grads, key_part, preferred_element_type=jnp.float32
        )

    grad_queries = over_blocks(
        advance,
        jnp.zeros((seq_count, head_count, HEAD_DIM, group_rows), jnp.float32),
        block_kv.shape[2],
        group_rows,
    )
    query_pack = jnp.concatenate(
        [
            query_heads.reshape(seq_count, group_width, group_rows),
            out_grads.reshape(seq_count, group_width, group_rows),
        ],
        axis=1,
    ).astype(jnp.float32)
    statistics = jnp.concatenate([log_sum, deltas], axis=1)

    def fold_keys(running, portion):
        block_pack, block_stats, block_pos = portion
        block_queries, block_outs = split_pairs(block_pack.astype(jnp.bfloat16), head_count)

        def advance(current, offset, extent):
            query_part = slice_last(block_queries, offset, extent)
            outs_part = slice_last(block_outs, offset, extent)
            stats_part = slice_last(block_stats, offset, extent)
            pos_part = slice_last(block_pos[:, 0], offset, extent)
            weights, score_grads = score_terms(
                query_part,
                outs_part,
                stats_part[:, :head_count],
                stats_part[:, head_count:],
                pos_part,
                own_keys,
                own_values,
                positions,
                slopes,
            )
            key_sum = current[0] + SCORE_SCALE * jnp.einsum(
                "shqk,shdq->shdk", score_grads, query_part, preferred_element_type=jnp.float32
            )
            value_sum = current[1] + jnp.einsum(
                "shqk,shdq->shdk", weights, outs_part, preferred_element_type=jnp.float32
            )
            return (key_sum, value_sum)

        return over_blocks(advance, running, block_pack.shape[2], group_rows)

    empty_grads = jnp.zeros((seq_count, head_count, HEAD_DIM, group_rows), jnp.float32)
    grad_keys, grad_values = fold_keys(
        (empty_grads, empty_grads),
        (
            lax.all_gather(query_pack.astype(jnp.bfloat16), "seq", axis=2, tiled=True).astype(
                jnp.float32
            ),
            lax.all_gather(statistics.astype(jnp.bfloat16), "seq", axis=2, tiled=True).astype(
                jnp.float32
            ),
            lax.all_gather(key_pos, "seq", axis=2, tiled=True),
        ),
    )
    grad_stack = jnp.stack(
        [
            grad_queries.reshape(seq_count, group_width, group_rows),
            grad_keys.reshape(seq_count, group_width, group_rows),
            grad_values.reshape(seq_count, group_width, group_rows),
        ],
        axis=1,
    ).astype(jnp.bfloat16)
    back_tokens = lax.all_to_all(
        grad_stack[:, :, None], "head", split_axis=4, concat_axis=2, tiled=True
    )
    grad_proj = back_tokens.reshape(seq_count, 3 * inner_width, row_count)
    column_sums = jnp.sum(grad_proj.astype(jnp.float32), axis=(0, 2))
    grad_qv = jnp.stack([column_sums[:inner_width], column_sums[2 * inner_width :]], axis=0)
    grad_w_qkv = jnp.einsum("std,sct->dc", tokens, grad_proj, preferred_element_type=jnp.float32)
    input_grad = first_grad + jnp.einsum(
        "sct,dc->std", grad_proj, qkv_full, preferred_element_type=jnp.float32
    )
    across = (
        lax.psum_scatter(grad_w_qkv, "seq", scatter_dimension=0, tiled=True),
        lax.psum_scatter(grad_qv, "seq", scatter_dimension=1, tiled=True),
        lax.psum_scatter(grad_w_attn, "seq", scatter_dimension=0, tiled=True),
        lax.psum_scatter(grad_attn_bias, "seq", scatter_dimension=0, tiled=True),
        lax.psum_scatter(grad_gain_one, "seq", scatter_dimension=0, tiled=True),
        lax.psum_scatter(grad_offset_one, "seq", scatter_dimension=0, tiled=True),
        lax.psum_scatter(grad_w_in, "seq", scatter_dimension=0, tiled=True),
        lax.psum_scatter(grad_in_bias, "seq", scatter_dimension=0, tiled=True),
        lax.psum_scatter(grad_w_out, "seq", scatter_dimension=0, tiled=True),
        lax.psum_scatter(grad_out_bias, "seq", scatter_dimension=0, tiled=True),
        lax.psum_scatter(grad_gain_two, "seq", scatter_dimension=0, tiled=True),
        lax.psum_scatter(grad_offset_two, "seq", scatter_dimension=0, tiled=True),
    )
    shares = (
        lax.psum_scatter(
            across[0].astype(jnp.bfloat16), "head", scatter_dimension=0, tiled=True
        ).astype(jnp.float32),
        lax.psum_scatter(
            across[1].astype(jnp.bfloat16), "head", scatter_dimension=1, tiled=True
        ).astype(jnp.float32),
        lax.psum_scatter(
            across[2].astype(jnp.bfloat16), "head", scatter_dimension=0, tiled=True
        ).astype(jnp.float32),
        lax.psum_scatter(
            across[3].astype(jnp.bfloat16), "head", scatter_dimension=0, tiled=True
        ).astype(jnp.float32),
        lax.psum_scatter(
            across[4].astype(jnp.bfloat16), "head", scatter_dimension=0, tiled=True
        ).astype(jnp.float32),
        lax.psum_scatter(
            across[5].astype(jnp.bfloat16), "head", scatter_dimension=0, tiled=True
        ).astype(jnp.float32),
        lax.psum_scatter(
            across[6].astype(jnp.bfloat16), "head", scatter_dimension=0, tiled=True
        ).astype(jnp.float32),
        lax.psum_scatter(
            across[7].astype(jnp.bfloat16), "head", scatter_dimension=0, tiled=True
        ).astype(jnp.float32),
        lax.psum_scatter(
            across[8].astype(jnp.bfloat16), "head", scatter_dimension=0, tiled=True
        ).astype(jnp.float32),
        lax.psum_scatter(
            across[9].astype(jnp.bfloat16), "head", scatter_dimension=0, tiled=True
        ).astype(jnp.float32),
        lax.psum_scatter(
            across[10].astype(jnp.bfloat16), "head", scatter_dimension=0, tiled=True
        ).astype(jnp.float32),
        lax.psum_scatter(
            across[11].astype(jnp.bfloat16), "head", scatter_dimension=0, tiled=True
        ).astype(jnp.float32),
    )
    return (
        result.astype(jnp.bfloat16),
        input_grad,
        shares[0],
        shares[1],
        shares[2],
        shares[3],
        shares[4],
        shares[5],
        shares[6],
        shares[7],
        shares[8],
        shares[9],
        shares[10],
        shares[11],
    )


def solution(mesh):
    placed = (
        P(None, ("seq", "head"), None),
        P(None, "seq"),
        P(("seq", "head"), None),
        P(None, ("seq", "head")),
        P(("seq", "head"), None),
        P(("seq", "head")),
        P(("seq", "head")),
        P(("seq", "head")),
        P(("seq", "head"), None),
        P(("seq", "head")),
        P(("seq", "head"), None),
        P(("seq", "head")),
        P(("seq", "head")),
        P(("seq", "head")),
        P(None, ("seq", "head"), None),
    )
    return jax.shard_map(
        body,
        mesh=mesh,
        in_specs=placed,
        out_specs=(
            P(None, ("seq", "head"), None),
            P(None, ("seq", "head"), None),
            P(("seq", "head"), None),
            P(None, ("seq", "head")),
            P(("seq", "head"), None),
            P(("seq", "head")),
            P(("seq", "head")),
            P(("seq", "head")),
            P(("seq", "head"), None),
            P(("seq", "head")),
            P(("seq", "head"), None),
            P(("seq", "head")),
            P(("seq", "head")),
            P(("seq", "head")),
        ),
        check_vma=False,
    )
```

profile of v0, /device:TPU:0, one launch (start us, length us, event | category | flops | bytes accessed | tf_op | source)
XLA Modules:
  0.0 1302.7 jit_solution(4569622715952971798)
XLA Ops:
  8.0 43.2 %all-gather.1 = bf16[32,24,2]{1,2,0:T(2,128)(2,1)S(1)} all-gather(bf16[1,24,2]{1,2,0:T(2,128)(2,1)} %bitcast.213), channel_id=1, replica_groups=mesh['seq'=8,'head'=4] {'seq','head'}, dimensions={0}, use_global_device_ids=true | all-gather | bytes 3168 | tf_op jit(solution)/shard_map/all_gather | solution.py:92
  51.4 22.4 %all-gather.9.cloned.1.call-done = bf16[768,2304]{1,0:T(8,128)(2,1)} async-done(((bf16[24,2304]{1,0:T(8,128)(2,1)}), bf16[768,2304]{1,0:T(8,128)(2,1)}) %all-gather.9.cloned.1.call-update) | async-done | bytes 3538960 | tf_op jit(solution)/shard_map/all_gather | solution.py:91
  73.8 2.6 fusion.64
  77.3 14.2 %all_to_all.63 = bf16[2,3,4,192,64]{3,4,1,0,2:T(8,128)(2,1)S(1)} all-to-all(bf16[2,3,4,192,64]{3,4,1,0,2:T(8,128)(2,1)S(1)} %copy.68), channel_id=1, replica_groups=mesh['seq'=8,'head'=4] {'head'}, dimensions={2} | all-to-all | bytes 1179648 | tf_op jit(solution)/shard_map/all_to_all | solution.py:112
  94.5 26.3 %all-gather = s32[2,2048]{1,0:T(2,128)S(1)} all-gather(s32[2,256]{1,0:T(2,128)} %param.22), channel_id=2, replica_groups=mesh['seq'=8,'head'=4] {'seq'}, dimensions={1}, use_global_device_ids=true | all-gather | bytes 18432 | tf_op jit(solution)/shard_map/all_gather | solution.py:123
  121.0 33.6 %all-gather.11.cloned.1.call-done = bf16[2,384,2048]{2,1,0:T(8,128)(2,1)} async-done(((bf16[2,384,256]{2,1,0:T(8,128)(2,1)}), bf16[2,384,2048]{2,1,0:T(8,128)(2,1)}) %all-gather.11.cloned.1.call-update) | async-done | bytes 3145744 | tf_op jit(solution)/shard_map/all_gather | solution.py:122
  154.6 4.0 slice_bitcast_fusion.2
  158.6 31.2 %while.48 = (s32[]{:T(128)}, f32[2,3,256]{2,1,0:T(4,128)S(1)}, f32[2,3,256]{2,1,0:T(4,128)S(1)}, f32[2,3,64,256]{3,2,1,0:T(8,128)S(1)}, bf16[2,3,64,2048]{3,2,1,...) while((s32[]{:T(128)}, f32[2,3,256]{2,1,0:T(4,128)S(1)}, ...), condition=%wide.region_3.0_spmd.clone, body=%wide.region_0.0_spmd.clone.sunk | while | flops 104504848 | bytes 7250151 | solution.py:55
  190.8 3.4 all-to-all-start.1
  196.0 39.4 %all-reduce.25 = (bf16[6144]{0:T(1024)(128)(2,1)S(1)}, bf16[768]{0:T(1024)(128)(2,1)S(1)}, bf16[768]{0:T(1024)(128)(2,1)S(1)}, bf16[768]{0:T(1024)(128)(2,1)S(1)...) all-reduce(bf16[6144]{0:T(1024)(128)(2,1)S(1)} %dynamic-update-slic, ...), channel_id=1, replica_groups=mesh['seq'=8,'head'=4] {'seq','head'}, use_global_device_ids=true, to_apply=%add.5 | all-reduce | flops 10752 | bytes 43008
  236.0 1.7 fusion.113
  238.0 55.6 %all-gather.15.cloned.1.call-done = bf16[768,6144]{1,0:T(8,128)(2,1)} async-done(((bf16[24,6144]{1,0:T(8,128)(2,1)}), bf16[768,6144]{1,0:T(8,128)(2,1)}) %all-gather.15.cloned.1.call-update) | async-done | bytes 9437200 | tf_op jit(solution)/shard_map/all_gather | solution.py:163
  293.5 5.1 fusion.53
  300.3 4.3 multiply_convert_fusion.1
  304.6 53.9 %all-gather.17.cloned.1.call-done = bf16[3072,768]{1,0:T(8,128)(2,1)} async-done(((bf16[96,768]{1,0:T(8,128)(2,1)}), bf16[3072,768]{1,0:T(8,128)(2,1)}) %all-gather.17.cloned.1.call-update) | async-done | bytes 4718608 | tf_op jit(solution)/shard_map/all_gather | solution.py:165
  358.5 3.4 fusion.114
  365.0 3.1 fusion.96
  368.1 6.1 multiply_reduce_fusion
  376.4 8.6 all_to_all.64
  386.0 1.9 convolution_bitcast_fusion.3
  390.2 6.0 convolution_bitcast_fusion.1
  399.1 57.3 %while.49 = (s32[]{:T(128)}, f32[2,3,64,256]{3,2,1,0:T(8,128)}, bf16[2,3,64,2048]{3,2,1,0:T(8,128)(2,1)}, bf16[2,3,64,256]{3,2,1,0:T(8,128)(2,1)S(1)}, s32[2,256...) while((s32[]{:T(128)}, f32[2,3,64,256]{3,2,1,0:T(8,128)}, ...), condition=%wide.region_14.0_spmd.clone, body=%wide.region_13.0_spmd.clone.sunk | while | flops 154435600 | bytes 9185612 | solution.py:55
  403.4 2.1 fusion.165
  410.5 2.1 fusion.165
  417.7 2.1 fusion.165
  424.8 2.1 fusion.165
  429.8 1.6 abs_convert_fusion.7
  432.0 2.1 fusion.165
  439.1 2.1 fusion.165
  446.2 2.1 fusion.165
  453.4 2.3 fusion.165
  456.4 1.7 convert.18
  458.8 31.0 %all_gather.66 = bf16[2,6,2048]{2,1,0:T(8,128)(2,1)S(1)} all-gather(bf16[2,6,256]{2,1,0:T(8,128)(2,1)S(1)} %pad_maximum_fusion.2), channel_id=1, replica_groups=mesh['seq'=8,'head'=4] {'seq'}, dimensions={2}, use_global_device_ids=true | all-gather | bytes 55296 | tf_op jit(solution)/shard_map/all_gather | solution.py:293
  490.5 4.7 copy.78
  495.2 4.0 slice_bitcast_fusion
  499.2 55.1 %while.50 = (s32[]{:T(128)}, f32[2,3,64,256]{3,2,1,0:T(8,128)S(1)}, f32[2,3,64,256]{3,2,1,0:T(8,128)S(1)}, bf16[2,3,64,2048]{3,2,1,0:T(8,128)(2,1)}, bf16[2,3,64...) while((s32[]{:T(128)}, f32[2,3,64,256]{3,2,1,0:T(8,128)S(1)}, ...), condition=%wide.region_16.0_spmd.clone, body=%wide.region_15.0_spmd.clone.sunk | while | flops 205357072 | bytes 8566537 | solution.py:55
  504.4 1.6 fusion.173
  511.3 1.6 fusion.173
  518.2 1.6 fusion.173
  525.1 1.6 fusion.173
  532.0 1.6 fusion.173
  538.9 1.6 fusion.173
  545.7 1.6 fusion.173
  552.6 1.7 fusion.173
  556.2 14.1 %all_to_all.65 = bf16[2,3,1,192,256]{3,0,2,1,4:T(2,128)(2,1)S(1)} all-to-all(bf16[2,3,1,192,256]{3,0,2,1,4:T(2,128)(2,1)S(1)} %copy.80), channel_id=1, replica_groups=mesh['seq'=8,'head'=4] {'head'}, dimensions={4} | all-to-all | bytes 1179648 | tf_op jit(solution)/shard_map/all_to_all | solution.py:307
  571.7 4.0 convolution_bitcast_fusion.2
  575.7 8.0 copy.86
  584.4 10.0 convolution_bitcast_fusion
  594.6 1.6 convert_element_type.264
  597.7 85.1 %reduce-scatter.25.cloned.1.call-done = f32[384,768]{1,0:T(8,128)} async-done(((f32[3072,768]{1,0:T(8,128)}), f32[384,768]{1,0:T(8,128)}) %reduce-scatter.25.cloned.1.call-update) | async-done | bytes 1179664 | tf_op jit(solution)/shard_map/reduce_scatter | solution.py:326
  682.7 2.1 convert_element_type.278
  685.0 129.6 %reduce-scatter.29.cloned.1.call-done = f32[96,2304]{1,0:T(8,128)} async-done(((f32[768,2304]{1,0:T(8,128)}), f32[96,2304]{1,0:T(8,128)}) %reduce-scatter.29.cloned.1.call-update) | async-done | bytes 884752
  817.4 313.8 %reduce-scatter.21.cloned.1.call-done = f32[96,6144]{1,0:T(8,128)} async-done(((f32[768,6144]{1,0:T(8,128)}), f32[96,6144]{1,0:T(8,128)}) %reduce-scatter.21.cloned.1.call-update) | async-done | bytes 2359312 | tf_op jit(solution)/shard_map/reduce_scatter | solution.py:324
  1131.2 2.8 convert_element_type.273
  1138.0 1.6 convert_reduce_fusion
  1139.7 35.8 %all-reduce.24 = (bf16[768]{0:T(1024)(128)(2,1)S(1)}, bf16[768]{0:T(1024)(128)(2,1)S(1)}, bf16[768]{0:T(1024)(128)(2,1)S(1)}, bf16[6144]{0:T(1024)(128)(2,1)S(1)...) all-reduce(f32[768]{0:T(1024)S(1)} %copy-done.28, ...), channel_id=9, replica_groups=mesh['seq'=8,'head'=4] {'seq'}, use_global_device_ids=true, to_apply=%region_25.0.clone | all-reduce | flops 10752 | bytes 64512
  1177.5 4.0 fusion.75
  1181.5 36.5 %reduce-scatter.33.cloned.1.call-done = f32[96,2]{1,0:T(8,128)} async-done(((f32[768,2]{1,0:T(8,128)}), f32[96,2]{1,0:T(8,128)}) %reduce-scatter.33.cloned.1.call-update) | async-done | bytes 784
  1218.9 5.7 all-reduce.26
  1227.7 14.7 %reduce-scatter.27.cloned.1.call-done = bf16[96,768]{1,0:T(8,128)(2,1)} async-done(((bf16[384,768]{1,0:T(8,128)(2,1)}), bf16[96,768]{1,0:T(8,128)(2,1)}) %reduce-scatter.27.cloned.1.call-update) | async-done | bytes 147472 | tf_op jit(solution)/shard_map/reduce_scatter | solution.py:356
  1242.4 1.6 convert_element_type.279
  1244.0 22.0 %reduce-scatter.31.cloned.1.call-done = bf16[24,2304]{1,0:T(8,128)(2,1)} async-done(((bf16[96,2304]{1,0:T(8,128)(2,1)}), bf16[24,2304]{1,0:T(8,128)(2,1)}) %reduce-scatter.31.cloned.1.call-update) | async-done | bytes 110608
  1268.3 26.1 %reduce-scatter.23.cloned.1.call-done = bf16[24,6144]{1,0:T(8,128)(2,1)} async-done(((bf16[96,6144]{1,0:T(8,128)(2,1)}), bf16[24,6144]{1,0:T(8,128)(2,1)}) %reduce-scatter.23.cloned.1.call-update) | async-done | bytes 294928 | tf_op jit(solution)/shard_map/reduce_scatter | solution.py:350
  1294.4 1.8 convert_element_type.274
  (436 shorter events, 150.6 us)
Async XLA Ops:
  7.2 66.6 %all-gather.9.cloned.1.call-start = ((), (), s32[]{:S(2)}) async-start(), calls=%async_computation.13 | async-start | bytes 3649536 | tf_op jit(solution)/shard_map/all_gather | solution.py:91
  7.9 146.7 %all-gather.11.cloned.1.call-start = ((), (), s32[]{:S(2)}) async-start(), calls=%async_computation.14 | async-start | bytes 3538944 | tf_op jit(solution)/shard_map/all_gather | solution.py:122
  92.6 143.4 %all-gather.13.cloned.1.call-start = ((), (), s32[]{:S(2)}) async-start(), calls=%async_computation.15 | async-start | bytes 1216512 | tf_op jit(solution)/shard_map/all_gather | solution.py:93
  93.3 200.2 %all-gather.15.cloned.1.call-start = ((), (), s32[]{:S(2)}) async-start(), calls=%async_computation.16 | async-start | bytes 9732096 | tf_op jit(solution)/shard_map/all_gather | solution.py:163
  93.9 264.6 %all-gather.17.cloned.1.call-start = ((), (), s32[]{:S(2)}) async-start(), calls=%async_computation.17 | async-start | bytes 4866048 | tf_op jit(solution)/shard_map/all_gather | solution.py:165
  189.8 46.2 %copy-start.14 = (f32[2,3,256]{2,1,0:T(4,128)}, f32[2,3,256]{2,1,0:T(4,128)S(1)}, u32[]{:S(2)}) copy-start(f32[2,3,256]{2,1,0:T(4,128)S(1)} %get-tuple-element.555) | copy-start | bytes 18436
  189.8 46.2 %copy-start.18 = (s32[2,1,2048]{2,0,1:T(2,128)}, s32[2,1,2048]{2,0,1:T(2,128)S(1)}, u32[]{:S(2)}) copy-start(s32[2,1,2048]{2,0,1:T(2,128)S(1)} %get-tuple-element.1288) | copy-start | bytes 49156
  189.8 4.5 copy-start.33
  189.8 4.7 copy-start.34
  189.9 5.0 copy-start.35
  189.9 5.2 copy-start.36
  189.9 5.4 copy-start.37
  189.9 5.6 copy-start.38
  189.9 5.8 copy-start.39
  189.9 46.1 %copy-start.11 = (bf16[2,64,768]{2,1,0:T(8,128)(2,1)S(1)}, bf16[2,64,768]{2,1,0:T(8,128)(2,1)}, u32[]{:S(2)}) copy-start(bf16[2,64,768]{2,1,0:T(8,128)(2,1)} %param.21) | copy-start | bytes 589828
  190.8 44.6 %all-to-all-start.1 = ((bf16[2,1,192,256]{2,0,1,3:T(2,128)(2,1)}), bf16[2,1,192,256]{2,0,1,3:T(2,128)(2,1)S(1)}, u32[]{:S(2)}, u32[]{:S(2)}) async-start(bf16[2,1,192,256]{2,0,1,3:T(2,128)(2,1)} %copy.72), calls=%async_computation.1 | async-start | bytes 524288 | tf_op jit(solution)/shard_map/all_to_all | solution.py:150
  194.3 296.3 %all-gather.19.cloned.1.call-start = ((), (), s32[]{:S(2)}) async-start(), calls=%async_computation.18 | async-start | bytes 3538944 | tf_op jit(solution)/shard_map/all_gather | solution.py:290
  237.7 136.4 %copy-start.19 = (f32[2,64]{1,0:T(2,128)}, f32[2,64]{1,0:T(2,128)S(1)}, u32[]{:S(2)}) copy-start(f32[2,64]{1,0:T(2,128)S(1)} %broadcast_multiply_fusion.1) | copy-start | bytes 1540
  237.9 136.2 %copy-start.21 = (f32[2,64]{1,0:T(2,128)}, f32[2,64]{1,0:T(2,128)S(1)}, u32[]{:S(2)}) copy-start(f32[2,64]{1,0:T(2,128)S(1)} %fusion.103) | copy-start | bytes 1540
  300.3 61.6 %copy-start.9 = (bf16[2,64,768]{2,1,0:T(8,128)(2,1)S(1)}, bf16[2,64,768]{2,1,0:T(8,128)(2,1)}, u32[]{:S(2)}) copy-start(bf16[2,64,768]{2,1,0:T(8,128)(2,1)} %param.35) | copy-start | bytes 589828
  358.5 6.5 copy-start.2
  358.5 6.5 copy-start.10
  358.5 6.5 copy-start.1
  358.5 9.6 slice-start
  358.5 9.6 slice-start.1
  365.0 3.1 copy-start.13
  365.0 3.1 slice-start.2
  368.1 6.1 copy-start.3
  374.4 2.0 copy-start.7
  386.0 208.6 %reduce-scatter.17.cloned.1.call-start = ((), (), s32[]{:S(2)}) async-start(), calls=%async_computation.19 | async-start | bytes 2654208 | tf_op jit(solution)/shard_map/reduce_scatter | solution.py:320
  387.9 294.8 %reduce-scatter.25.cloned.1.call-start = ((), (), s32[]{:S(2)}) async-start(), calls=%async_computation.23 | async-start | bytes 10616832 | tf_op jit(solution)/shard_map/reduce_scatter | solution.py:326
  396.3 418.3 %reduce-scatter.29.cloned.1.call-start = ((), (), s32[]{:S(2)}) async-start(), calls=%async_computation.25 | async-start | bytes 7962624
  399.1 4.3 copy-start.16
  403.4 2.9 copy-start.24
  406.3 4.2 copy-start.16
  410.5 2.9 copy-start.24
  413.4 4.3 copy-start.16
  417.7 2.9 copy-start.24
  420.6 4.2 copy-start.16
  424.8 2.9 copy-start.24
  427.7 4.2 copy-start.16
  432.0 2.9 copy-start.24
  434.8 4.2 copy-start.16
  439.1 2.9 copy-start.24
  442.0 4.2 copy-start.16
  446.2 2.9 copy-start.24
  449.1 4.2 copy-start.16
  453.4 3.0 copy-start.24
  583.8 547.5 %reduce-scatter.21.cloned.1.call-start = ((), (), s32[]{:S(2)}) async-start(), calls=%async_computation.21 | async-start | bytes 21233664 | tf_op jit(solution)/shard_map/reduce_scatter | solution.py:324
  594.5 581.6 %reduce-scatter.19.cloned.1.call-start = ((), (), s32[]{:S(2)}) async-start(), calls=%async_computation.20 | async-start | bytes 184320 | tf_op jit(solution)/shard_map/reduce_scatter | solution.py:338
  596.2 621.8 %reduce-scatter.33.cloned.1.call-start = ((), (), s32[]{:S(2)}) async-start(), calls=%async_computation.27 | async-start | bytes 442368
  597.6 644.8 %reduce-scatter.27.cloned.1.call-start = ((), (), s32[]{:S(2)}) async-start(), calls=%async_computation.24 | async-start | bytes 737280 | tf_op jit(solution)/shard_map/reduce_scatter | solution.py:356
  684.9 581.2 %reduce-scatter.31.cloned.1.call-start = ((), (), s32[]{:S(2)}) async-start(), calls=%async_computation.26 | async-start | bytes 552960
  817.1 317.0 %copy-start.41 = (u32[32]{0:T(128)S(1)}, u32[32]{0:T(128)}, u32[]{:S(2)}) copy-start(u32[32]{0:T(128)} %constant.272) | copy-start | bytes 388
  817.1 318.9 %copy-start.40 = (u32[32]{0:T(128)S(1)}, u32[32]{0:T(128)}, u32[]{:S(2)}) copy-start(u32[32]{0:T(128)} %constant.268) | copy-start | bytes 388
  817.1 320.8 %copy-start.4 = (f32[2,64,3072]{2,1,0:T(8,128)S(1)}, f32[2,64,3072]{2,1,0:T(8,128)}, u32[]{:S(2)}) copy-start(f32[2,64,3072]{2,1,0:T(8,128)} %copy-done.3) | copy-start | bytes 4718596
  817.1 477.2 %reduce-scatter.23.cloned.1.call-start = ((), (), s32[]{:S(2)}) async-start(), calls=%async_computation.22 | async-start | bytes 1474560 | tf_op jit(solution)/shard_map/reduce_scatter | solution.py:350
  1137.9 1.7 copy-start.25
  1137.9 1.7 copy-start.26
  1137.9 1.7 copy-start.27
  1137.9 1.7 copy-start.28
  1137.9 1.7 copy-start.31
  1137.9 39.5 %copy-start.8 = (f32[2,64,768]{2,1,0:T(8,128)S(1)}, f32[2,64,768]{2,1,0:T(8,128)}, u32[]{:S(2)}) copy-start(f32[2,64,768]{2,1,0:T(8,128)} %copy-done.7) | copy-start | bytes 1179652
  1138.0 39.5 %copy-start.30 = (f32[2,64]{1,0:T(2,128)S(1)}, f32[2,64]{1,0:T(2,128)}, u32[]{:S(2)}) copy-start(f32[2,64]{1,0:T(2,128)} %copy-done.29) | copy-start | bytes 1540
  (25 other events, 28.2 us)
Sparse Core Ops, SparseCore 0:
  10.9 62.8 all-gather.8
  92.7 61.7 all-gather.10
  157.5 52.4 all-gather.12
  212.8 80.6 all-gather.14
  296.3 62.1 all-gather.16
  386.1 59.0 all-gather.18
  448.7 67.8 reduce-scatter.16
  520.2 162.5 reduce-scatter.24
  686.4 128.1 reduce-scatter.28
  818.8 312.3 reduce-scatter.20
  1134.4 18.7 reduce-scatter.18
  1156.7 61.3 reduce-scatter.32
  1221.3 21.0 reduce-scatter.26
  1244.9 21.0 reduce-scatter.30
  1268.7 25.6 reduce-scatter.22
where the time goes:
time: 1310 us; the launch traced here: 1300 us
  waiting for transfers between devices  796 us (61%)
  blocking collectives  218 us (17%)
  matrix products  134 us (10%)
  local copies, waits for them, and re-layouts  66.3 us (5%)
  other arithmetic  64.9 us (5%)
  between operations  17.4 us (1%)
    reduce_scatter x1, waiting for transfers between devices, body(): lax.psum_scatter(grad_w_in, 'seq', scatter_dimension=0, tiled=True)  314 us
    unnamed x18, waiting for transfers between devices  191 us
    reduce_scatter x1, waiting for transfers between devices, body(): lax.psum_scatter(grad_w_out, 'seq', scatter_dimension=0, tiled=True)  85.1 us
    unnamed x3, blocking collectives  81 us
    all_gather x1, waiting for transfers between devices, body(): lax.all_gather(w_in, ('seq', 'head'), axis=0, tiled=True)  55.6 us
    all_gather x1, waiting for transfers between devices, body(): lax.all_gather(w_out, ('seq', 'head'), axis=0, tiled=True)  53.9 us
    all_gather x1, blocking collectives, body(): lax.all_gather(qv_bias, ('seq', 'head'), axis=1, tiled=True)  43.2 us
    dot_general x24, matrix products, alibi_scores(): jnp.einsum('shdq,shdk->shqk', query_heads, key_heads, preferred_element_t...  34.8 us
  transfers between devices with their start and end apart: 16, of which 11 were waited for; matrix products, arithmetic and copies ran while one was open for 18% of the time, Pallas kernels for 0%

commit v1 on v0

v1 whole, which is shorter than its diff:
```python
import jax
import jax.numpy as jnp
from jax import lax
from jax.experimental import pallas as pl
from jax.experimental.pallas import tpu as pltpu
from jax.sharding import Mesh
from jax.sharding import PartitionSpec as P

HEADS = 12
HEAD_DIM = 64
GROUPS = 4
GROUP_HEADS = HEADS // GROUPS
GROUP_WIDTH = GROUP_HEADS * HEAD_DIM
EPSILON = 1e-12
SCORE_SCALE = 0.125
LOG2E = 1.4426950408889634
LOWEST = -1e30
KEY_BLOCK = 512
SEQ_GROUP = ("s", "g")
TOKEN_GROUP = ("y", "c")
CHUNKS = ("e", "y", "c")
SEQ_AXIS = ("s", "e", "g")
EVERY = ("s", "e", "g", "y", "c")
SWAP = ((0, 1), (1, 0))
BF16 = jnp.bfloat16
F32 = jnp.float32
VMEM_BYTES = 60 * 2**20


def nt(a, b):
    return lax.dot_general(a, b, (((1,), (1,)), ((), ())), preferred_element_type=F32)


def tn(a, b):
    return lax.dot_general(a, b, (((0,), (0,)), ((), ())), preferred_element_type=F32)


def nn(a, b):
    return lax.dot_general(a, b, (((1,), (0,)), ((), ())), preferred_element_type=F32)


def head_cols(head, base=0):
    return slice(base + head * HEAD_DIM, base + (head + 1) * HEAD_DIM)


def log2_scores(keys, queries, slope, key_pos, query_pos):
    products = nt(keys, queries)
    distances = jnp.abs(key_pos * slope - query_pos * slope)
    return products * (SCORE_SCALE * LOG2E) - distances


def attend_kernel(slopes_ref, q_ref, kv_ref, pq_ref, pk_ref, low_ref, out_ref, lse_ref):
    rows = q_ref.shape[0]
    blocks = kv_ref.shape[0] // KEY_BLOCK
    query_pos = pq_ref[...]
    for head in range(GROUP_HEADS):
        slope = slopes_ref[head]
        queries = q_ref[:, head_cols(head)]

        def visit(block, carry):
            top, total, summed = carry
            at = pl.ds(pl.multiple_of(block * KEY_BLOCK, KEY_BLOCK), KEY_BLOCK)
            keys = kv_ref[at, head_cols(head)]
            values = kv_ref[at, head_cols(head, GROUP_WIDTH)]
            scores = log2_scores(keys, queries, slope, pk_ref[at, :], query_pos)
            new_top = jnp.maximum(top, jnp.max(scores, axis=0, keepdims=True))
            weights = jnp.exp2(scores - new_top)
            shrink = jnp.exp2(top - new_top)
            total = total * shrink + jnp.sum(weights, axis=0, keepdims=True)
            summed = summed * shrink + tn(values, weights.astype(BF16))
            return new_top, total, summed

        top, total, summed = lax.fori_loop(
            0,
            blocks,
            visit,
            (
                jnp.full((1, rows), LOWEST, F32),
                jnp.zeros((1, rows), F32),
                jnp.zeros((HEAD_DIM, rows), F32),
            ),
        )
        attended = summed / total
        out_ref[head_cols(head), :] = attended
        low_ref[:, head_cols(head)] = attended.T.astype(BF16)
        lse_ref[head : head + 1, :] = top + jnp.log2(total)


def attend(slopes, queries, key_values, query_pos, key_pos):
    rows, length = queries.shape[0], key_values.shape[0]
    vmem = pl.BlockSpec(memory_space=pltpu.VMEM)
    return pl.pallas_call(
        attend_kernel,
        out_shape=(
            jax.ShapeDtypeStruct((rows, GROUP_WIDTH), BF16),
            jax.ShapeDtypeStruct((GROUP_WIDTH, rows), F32),
            jax.ShapeDtypeStruct((GROUP_HEADS, rows), F32),
        ),
        in_specs=[pl.BlockSpec(memory_space=pltpu.SMEM)] + [vmem] * 4,
        out_specs=(vmem,) * 3,
        compiler_params=pltpu.CompilerParams(vmem_limit_bytes=VMEM_BYTES),
        cost_estimate=pl.CostEstimate(
            flops=4 * rows * length * GROUP_WIDTH,
            bytes_accessed=rows * length,
            transcendentals=rows * length * GROUP_HEADS,
        ),
        name="attend",
    )(slopes, queries, key_values, query_pos, key_pos)


def attend_back_kernel(
    slopes_ref, q_ref, kv_ref, pq_ref, pk_ref, do_ref, out_ref, lse_ref, dq_ref, dkv_ref
):
    rows = q_ref.shape[0]
    blocks = kv_ref.shape[0] // KEY_BLOCK
    query_pos = pq_ref[...]
    for head in range(GROUP_HEADS):
        slope = slopes_ref[head]
        queries = q_ref[:, head_cols(head)]
        out_grads = do_ref[:, head_cols(head)]
        log_sum = lse_ref[head : head + 1, :]
        delta = jnp.sum(
            out_grads.astype(F32).T * out_ref[head_cols(head), :], axis=0, keepdims=True
        )

        def visit(block, query_grads):
            at = pl.ds(pl.multiple_of(block * KEY_BLOCK, KEY_BLOCK), KEY_BLOCK)
            keys = kv_ref[at, head_cols(head)]
            values = kv_ref[at, head_cols(head, GROUP_WIDTH)]
            scores = log2_scores(keys, queries, slope, pk_ref[at, :], query_pos)
            probs = jnp.exp2(scores - log_sum)
            prob_grads = nt(values, out_grads)
            score_grads = (probs * (prob_grads - delta)).astype(BF16)
            dkv_ref[at, head_cols(head, GROUP_WIDTH)] = nn(
                probs.astype(BF16), out_grads
            ).astype(BF16)
            dkv_ref[at, head_cols(head)] = (nn(score_grads, queries) * SCORE_SCALE).astype(BF16)
            return query_grads + tn(keys, score_grads)

        query_grads = lax.fori_loop(0, blocks, visit, jnp.zeros((HEAD_DIM, rows), F32))
        dq_ref[:, head_cols(head)] = (query_grads * SCORE_SCALE).T.astype(BF16)


def attend_back(slopes, queries, key_values, query_pos, key_pos, out_grads, attended, log_sums):
    rows, length = queries.shape[0], key_values.shape[0]
    vmem = pl.BlockSpec(memory_space=pltpu.VMEM)
    return pl.pallas_call(
        attend_back_kernel,
        out_shape=(
            jax.ShapeDtypeStruct((rows, GROUP_WIDTH), BF16),
            jax.ShapeDtypeStruct((length, 2 * GROUP_WIDTH), BF16),
        ),
        in_specs=[pl.BlockSpec(memory_space=pltpu.SMEM)] + [vmem] * 7,
        out_specs=(vmem,) * 2,
        compiler_params=pltpu.CompilerParams(vmem_limit_bytes=VMEM_BYTES),
        cost_estimate=pl.CostEstimate(
            flops=10 * rows * length * GROUP_WIDTH,
            bytes_accessed=rows * length,
            transcendentals=rows * length * GROUP_HEADS,
        ),
        name="attend_back",
    )(slopes, queries, key_values, query_pos, key_pos, out_grads, attended, log_sums)


def layer_norm(values, gain_vec, offsets):
    average = jnp.mean(values, axis=-1, keepdims=True)
    centred = values - average
    variance = jnp.mean(centred * centred, axis=-1, keepdims=True)
    return centred * lax.rsqrt(variance + EPSILON) * gain_vec + offsets


def geglu(joined):
    half_width = joined.shape[-1] // 2
    return (
        jax.nn.gelu(joined[..., :half_width], approximate=False) * joined[..., half_width:]
    )


def gather_group(block):
    pair = jnp.concatenate([block, lax.ppermute(block, "y", SWAP)])
    return jnp.concatenate([pair, lax.ppermute(pair, "c", SWAP)])


def sum_group(parts):
    half = parts.shape[0] // 2
    quarter = half // 2
    pair = parts[:half].astype(F32) + lax.ppermute(
        parts[half:].astype(BF16), "c", SWAP
    ).astype(F32)
    return pair[:quarter] + lax.ppermute(pair[quarter:].astype(BF16), "y", SWAP).astype(F32)


def body(
    tokens,
    positions,
    w_qkv,
    qv_bias,
    w_attn_out,
    attn_out_bias,
    norm1_gain,
    norm1_bias,
    w_in,
    in_bias,
    w_out,
    out_bias,
    norm2_gain,
    norm2_bias,
    cotangent,
):
    seq_count, row_count, width = tokens.shape
    outer = lax.axis_size("e")
    seq_size = 2 * outer * GROUPS
    devices = seq_size * 4
    shard = w_qkv.shape[0]
    ff_shard = w_out.shape[0]
    group = lax.axis_index("g")
    place = lax.axis_index("y") * 2 + lax.axis_index("c")
    qkv_cols = 3 * GROUP_WIDTH

    with jax.named_scope("gather_tokens"):
        spread = jnp.broadcast_to(
            tokens[:, None], (2, GROUPS, row_count, width)
        ).reshape(8, row_count, width)
        chunk = lax.all_to_all(spread, SEQ_GROUP, 0, 0, tiled=True).reshape(8 * row_count, width)

    small_parts = [
        qv_bias.reshape(-1),
        attn_out_bias,
        norm1_gain,
        norm1_bias,
        out_bias,
        norm2_gain,
        norm2_bias,
        in_bias,
    ]
    small_sizes = [part.shape[0] for part in small_parts]
    small_total = sum(small_sizes)
    extra = -(-(small_total + 2 * row_count) // shard)
    wide = -(-(qkv_cols + extra) // 128) * 128
    spare = wide - qkv_cols

    with jax.named_scope("gather_qkv_weights"):
        own_pos = lax.dynamic_slice_in_dim(positions, place * row_count, row_count, 1)
        pos_parts = jnp.concatenate([own_pos >> 7, own_pos & 127], axis=1).astype(BF16)
        filling = jnp.zeros((2, shard * spare - small_total - 2 * row_count), BF16)
        smalls = jnp.concatenate(small_parts)
        row = jnp.concatenate(
            [pos_parts, jnp.broadcast_to(smalls, (2, small_total)), filling], axis=1
        ).reshape(2, 1, shard, spare)
        columns = (
            w_qkv.reshape(shard, 3, GROUPS, GROUP_WIDTH)
            .transpose(2, 0, 1, 3)
            .reshape(1, GROUPS, shard, qkv_cols)
        )
        parcel = jnp.concatenate(
            [
                jnp.broadcast_to(columns, (2, GROUPS, shard, qkv_cols)),
                jnp.broadcast_to(row, (2, GROUPS, shard, spare)),
            ],
            axis=3,
        ).reshape(8, shard, wide)
        parcel = lax.all_to_all(parcel, SEQ_GROUP, 0, 0, tiled=True)
        parcels = lax.all_gather(parcel, CHUNKS, axis=0, tiled=False).reshape(
            outer, 2, 2, 2, GROUPS, shard, wide
        )
        qkv_slice = (
            parcels[..., :qkv_cols].transpose(3, 0, 4, 1, 2, 5, 6).reshape(width, qkv_cols)
        )
        vectors = parcels[..., qkv_cols:].reshape(outer, 2, 2, 2, GROUPS, shard * spare)

        def vector(number):
            at = 2 * row_count + sum(small_sizes[:number])
            return (
                vectors[..., at : at + small_sizes[number]]
                .transpose(3, 0, 4, 1, 2, 5)
                .reshape(devices, small_sizes[number])
            )

        qv_full = vector(0).reshape(devices, 2, shard).transpose(1, 0, 2).reshape(2, width)
        attn_bias, first_gain, first_offset, out_shift, second_gain, second_offset, in_shift = (
            vector(number).reshape(-1).astype(F32) for number in range(1, 8)
        )
        chunk_pos = (
            vectors[..., :row_count].astype(F32) * 128.0
            + vectors[..., row_count : 2 * row_count].astype(F32)
        ).reshape(outer, 2, 2, 8 * row_count)

    with jax.named_scope("gather_ff_weights"):
        in_parts = (
            w_in.reshape(shard, 2 * seq_size, 4, ff_shard)
            .transpose(2, 0, 1, 3)
            .reshape(4, shard, 2 * seq_size * ff_shard)
        )
        in_parts = lax.all_to_all(in_parts, TOKEN_GROUP, 0, 0, tiled=True)
        in_slice = lax.all_gather(
            in_parts.reshape(4 * shard, 2 * seq_size * ff_shard), SEQ_AXIS, axis=0, tiled=True
        )
        out_slice = lax.all_gather(w_out, SEQ_AXIS, axis=0, tiled=True)
        attn_full = lax.all_gather(w_attn_out, EVERY, axis=0, tiled=True)
        in_shift_slice = lax.dynamic_index_in_dim(
            in_shift.reshape(2 * seq_size, 4, ff_shard), place, 1, keepdims=False
        ).reshape(-1)

    with jax.named_scope("project"):
        qv_slice = lax.dynamic_slice_in_dim(qv_full, group * GROUP_WIDTH, GROUP_WIDTH, 1).astype(
            F32
        )
        column_bias = jnp.concatenate(
            [qv_slice[0], jnp.zeros((GROUP_WIDTH,), F32), qv_slice[1]]
        )
        qkv = (
            jnp.dot(chunk, qkv_slice, preferred_element_type=F32) + column_bias
        ).astype(BF16)
        queries, own_kv = qkv[:, :GROUP_WIDTH], qkv[:, GROUP_WIDTH:]
    with jax.named_scope("gather_kv"):
        spans = [own_kv]
        if outer > 1:
            spans = [lax.all_gather(own_kv, "e", axis=0, tiled=True)]
        key_values = gather_group(spans[0])
    y_at, c_at = lax.axis_index("y"), lax.axis_index("c")
    ordered_pos = jnp.stack(
        [
            lax.dynamic_index_in_dim(
                lax.dynamic_index_in_dim(chunk_pos, y_at ^ ky, 1, keepdims=False),
                c_at ^ kc,
                1,
                keepdims=False,
            )
            for kc in (0, 1)
            for ky in (0, 1)
        ]
    )
    query_pos = lax.dynamic_index_in_dim(ordered_pos[0], lax.axis_index("e"), 0, keepdims=True)[0]
    query_pos = query_pos.reshape(1, -1)
    key_pos = ordered_pos.reshape(-1, 1)
    head_ids = group * GROUP_HEADS + jnp.arange(GROUP_HEADS)
    slopes = 2.0 ** (-8.0 * (head_ids + 1).astype(F32) / HEADS) * LOG2E

    with jax.named_scope("attention"):
        attended_low, attended, log_sums = attend(slopes, queries, key_values, query_pos, key_pos)

    with jax.named_scope("return_attended"):
        returned = lax.all_to_all(
            attended_low.reshape(8, row_count, GROUP_WIDTH), SEQ_GROUP, 0, 0, tiled=True
        )
        mixed = (
            returned.reshape(2, GROUPS, row_count, GROUP_WIDTH)
            .transpose(0, 2, 1, 3)
            .reshape(2 * row_count, width)
        )
    with jax.named_scope("first_norm"):
        rows = tokens.reshape(2 * row_count, width)
        attn_lin = jnp.dot(mixed, attn_full, preferred_element_type=F32) + attn_bias
        hidden, first_back = jax.vjp(
            layer_norm, rows.astype(F32) + attn_lin, first_gain, first_offset
        )
        hidden_low = hidden.astype(BF16)
    with jax.named_scope("gather_hidden"):
        hidden_group = gather_group(hidden_low)
    with jax.named_scope("ff_forward"):
        joined = jnp.dot(hidden_group, in_slice, preferred_element_type=F32) + in_shift_slice
        activated, gate_back = jax.vjp(geglu, joined)
        activated_low = activated.astype(BF16)
        ff_parts = jnp.dot(activated_low, out_slice, preferred_element_type=F32)
    with jax.named_scope("sum_ff"):
        ff_lin = sum_group(ff_parts) + out_shift
    with jax.named_scope("second_norm"):
        result, second_back = jax.vjp(layer_norm, hidden + ff_lin, second_gain, second_offset)
        second_grad, grad_gain_two, grad_offset_two = second_back(
            cotangent.reshape(2 * row_count, width).astype(F32)
        )
        ff_grad = second_grad.astype(BF16)
        grad_out_bias = jnp.sum(ff_grad.astype(F32), axis=0)
    with jax.named_scope("gather_ff_grad"):
        ff_grads = gather_group(ff_grad)
    with jax.named_scope("ff_backward"):
        act_grad = nt(ff_grads, out_slice)
        joined_grad = gate_back(act_grad)[0].astype(BF16)
        hidden_parts = nt(joined_grad, in_slice)
    with jax.named_scope("sum_hidden_grad"):
        hidden_grad = second_grad + sum_group(hidden_parts)
    with jax.named_scope("ff_weight_grads"):
        grad_out_slice = tn(activated_low, ff_grads).astype(BF16)
        grad_in_slice = tn(hidden_group, joined_grad).astype(BF16)
        grad_in_shift = jnp.sum(joined_grad.astype(F32), axis=0)
        grad_w_out = lax.psum_scatter(
            grad_out_slice, SEQ_AXIS, scatter_dimension=0, tiled=True
        ).astype(F32)
        grad_in_rows = lax.psum_scatter(
            grad_in_slice, SEQ_AXIS, scatter_dimension=0, tiled=True
        )
        grad_in_parts = lax.all_to_all(
            grad_in_rows.reshape(4, shard, 2 * seq_size * ff_shard), TOKEN_GROUP, 0, 0, tiled=True
        )
        grad_w_in = (
            grad_in_parts.reshape(4, shard, 2 * seq_size, ff_shard)
            .transpose(1, 2, 0, 3)
            .reshape(shard, 2 * devices * ff_shard)
            .astype(F32)
        )
    with jax.named_scope("first_norm_back"):
        first_grad, grad_gain_one, grad_offset_one = first_back(hidden_grad)
        attn_grad = first_grad.astype(BF16)
        grad_attn_bias = jnp.sum(attn_grad.astype(F32), axis=0)
        out_grad = nt(attn_grad, attn_full).astype(BF16)
    with jax.named_scope("send_out_grad"):
        out_grads = lax.all_to_all(
            out_grad.reshape(2, row_count, GROUPS, GROUP_WIDTH)
            .transpose(0, 2, 1, 3)
            .reshape(8, row_count, GROUP_WIDTH),
            SEQ_GROUP,
            0,
            0,
            tiled=True,
        ).reshape(8 * row_count, GROUP_WIDTH)
    with jax.named_scope("attn_weight_grad"):
        grad_attn = (
            tn(mixed, attn_grad)
            .astype(BF16)
            .reshape(seq_size, 4, shard, width)
            .transpose(1, 0, 2, 3)
            .reshape(width, width)
        )
        grad_attn = lax.psum_scatter(grad_attn, TOKEN_GROUP, scatter_dimension=0, tiled=True)
        grad_w_attn = lax.psum_scatter(
            grad_attn, SEQ_AXIS, scatter_dimension=0, tiled=True
        ).astype(F32)

    with jax.named_scope("attention_back"):
        query_grads, kv_parts = attend_back(
            slopes, queries, key_values, query_pos, key_pos, out_grads, attended, log_sums
        )
    with jax.named_scope("sum_kv_grads"):
        kv_grads = sum_group(kv_parts)
        if outer > 1:
            kv_grads = lax.psum_scatter(kv_grads, "e", scatter_dimension=0, tiled=True)
        qkv_grad = jnp.concatenate([query_grads, kv_grads.astype(BF16)], axis=1)

    with jax.named_scope("input_grad"):
        input_parts = nt(qkv_grad, qkv_slice).astype(BF16).reshape(8, row_count, width)
        input_parts = lax.all_to_all(input_parts, SEQ_GROUP, 0, 0, tiled=True)
        input_grad = first_grad.reshape(2, row_count, width) + jnp.sum(
            input_parts.reshape(2, GROUPS, row_count, width).astype(F32), axis=1
        )
    with jax.named_scope("qkv_weight_grad"):
        grad_qkv_cols = tn(chunk, qkv_grad)
        column_sums = jnp.sum(qkv_grad.astype(F32), axis=0)
        grad_qv = lax.dynamic_update_slice(
            jnp.zeros((2, width), F32),
            jnp.stack([column_sums[:GROUP_WIDTH], column_sums[2 * GROUP_WIDTH :]]),
            (0, group * GROUP_WIDTH),
        )
        grad_in_bias = lax.dynamic_update_slice(
            jnp.zeros((2 * seq_size, 4, ff_shard), F32),
            grad_in_shift.reshape(2 * seq_size, 1, ff_shard),
            (0, place, 0),
        )
        small_grads = jnp.concatenate(
            [
                grad_qv.reshape(2, devices, shard).transpose(1, 0, 2).reshape(devices, 2 * shard),
                grad_attn_bias.reshape(devices, shard),
                grad_gain_one.reshape(devices, shard),
                grad_offset_one.reshape(devices, shard),
                grad_out_bias.reshape(devices, shard),
                grad_gain_two.reshape(devices, shard),
                grad_offset_two.reshape(devices, shard),
                grad_in_bias.reshape(devices, 2 * ff_shard),
                jnp.zeros((devices, shard * spare - small_total), F32),
            ],
            axis=1,
        ).reshape(devices, shard, spare)
        bundle = jnp.concatenate(
            [grad_qkv_cols.reshape(devices, shard, qkv_cols), small_grads], axis=2
        ).reshape(2 * seq_size, 2, shard, wide)
        keep = lax.dynamic_index_in_dim(bundle, c_at, 1, keepdims=False)
        give = lax.dynamic_index_in_dim(bundle, 1 - c_at, 1, keepdims=False).astype(BF16)
        keep = keep + lax.ppermute(give, "c", SWAP).astype(F32)
        shares = lax.all_to_all(
            keep.astype(BF16), ("s", "e", "g", "y"), 0, 0, tiled=True
        ).astype(F32)
        grad_w_qkv = (
            jnp.sum(
                shares[..., :qkv_cols].reshape(2 * outer, GROUPS, 2, shard, 3, GROUP_WIDTH),
                axis=(0, 2),
            )
            .transpose(1, 2, 0, 3)
            .reshape(shard, 3 * width)
        )
        totals = jnp.sum(shares[..., qkv_cols:], axis=0).reshape(-1)
        vectors_out = []
        at = 0
        for size in small_sizes:
            vectors_out.append(totals[at : at + size])
            at += size

    return (
        result.reshape(2, row_count, width).astype(BF16),
        input_grad,
        grad_w_qkv,
        vectors_out[0].reshape(2, shard),
        grad_w_attn,
        vectors_out[1],
        vectors_out[2],
        vectors_out[3],
        grad_w_in,
        vectors_out[7],
        grad_w_out,
        vectors_out[4],
        vectors_out[5],
        vectors_out[6],
    )


def solution(mesh):
    seq_size = mesh.shape["seq"]
    split = Mesh(mesh.devices.reshape(2, seq_size // 8, 4, 2, 2), EVERY)
    tokens_at = P(None, EVERY, None)
    rows_at = P(EVERY, None)
    vector_at = P(EVERY)
    return jax.shard_map(
        body,
        mesh=split,
        in_specs=(
            tokens_at,
            P(None, SEQ_AXIS),
            rows_at,
            P(None, EVERY),
            rows_at,
            vector_at,
            vector_at,
            vector_at,
            rows_at,
            vector_at,
            rows_at,
            vector_at,
            vector_at,
            vector_at,
            tokens_at,
        ),
        out_specs=(
            tokens_at,
            tokens_at,
            rows_at,
            P(None, EVERY),
            rows_at,
            vector_at,
            vector_at,
            vector_at,
            rows_at,
            vector_at,
            rows_at,
            vector_at,
            vector_at,
            vector_at,
        ),
        check_vma=False,
    )
```

time: 1310 us -> 457 us (0.35)
  waiting for transfers between devices: 796 us -> 269 us
  blocking collectives: 218 us -> 23.8 us
  matrix products: 134 us -> 23.5 us
  other arithmetic: 64.9 us -> 23.1 us
  starting transfers between devices: 4.5 us -> 38.1 us
  local copies, waits for them, and re-layouts: 66.3 us -> 37.3 us
  Pallas kernels: 0 us -> 25.6 us
    reduce_scatter x6 -> x4, waiting for transfers between devices: 440 us -> 143 us  [the longest x1 65.4 us: body(): lax.psum_scatter(grad_in_slice, SEQ_AXIS, scatter_dimension=0, tiled=True)]
    unnamed x18 -> x7, waiting for transfers between devices: 191 us -> 2.1 us
    all_gather x6 -> x3, waiting for transfers between devices: 165 us -> 41.4 us  [the longest x1 33.3 us: body(): out_slice = lax.all_gather(w_out, SEQ_AXIS, axis=0, tiled=True)]
    dot_general x68 -> x12, matrix products: 134 us -> 23.5 us  [the longest x4 9.11 us: tn(): lax.dot_general(a, b, (((0,), (0,)), ((), ())), preferred_element_type=F32)]
    all_gather x3 -> x1, blocking collectives: 101 us -> 8.87 us  [body(): lax.all_gather(parcel, CHUNKS, axis=0, tiled=False)]
    unnamed x3 -> x0, blocking collectives: 81 us -> none
    all_to_all x1 -> x7, waiting for transfers between devices: 0.01 us -> 43.9 us  [the longest x1 12.4 us: body(): input_parts = lax.all_to_all(input_parts, SEQ_GROUP, 0, 0, tiled=True)]
    ppermute x0 -> x13, waiting for transfers between devices: none -> 38 us  [the longest x3 17.1 us: gather_group(): pair = jnp.concatenate([block, lax.ppermute(block, 'y', SWAP)])]
  transfers between devices with their start and end apart: 16 -> 27, of which waited for: 11 -> 22; matrix products, arithmetic and copies ran while one was open for 18% -> 13% of each run, Pallas kernels for 0% -> 6%
where the time goes in v1:
time: 457 us; the launch traced here: 455 us
  waiting for transfers between devices  269 us (59%)
  starting transfers between devices  38.1 us (8%)
  local copies, waits for them, and re-layouts  37.3 us (8%)
  Pallas kernels  25.6 us (6%)
  blocking collectives  23.8 us (5%)
  matrix products  23.5 us (5%)
  other arithmetic  23.1 us (5%)
  between operations  15.4 us (3%)
    reduce_scatter x1, waiting for transfers between devices, body(): lax.psum_scatter(grad_in_slice, SEQ_AXIS, scatter_dimension=0, tiled=True)  65.4 us
    reduce_scatter x1, waiting for transfers between devices, body(): lax.psum_scatter(grad_attn, SEQ_AXIS, scatter_dimension=0, tiled=True)  57.4 us
    all_gather x1, waiting for transfers between devices, body(): out_slice = lax.all_gather(w_out, SEQ_AXIS, axis=0, tiled=True)  33.3 us
    reduce_scatter x1, waiting for transfers between devices, body(): lax.psum_scatter(grad_out_slice, SEQ_AXIS, scatter_dimension=0, tiled=True)  20.3 us
    ppermute x3, waiting for transfers between devices, gather_group(): pair = jnp.concatenate([block, lax.ppermute(block, 'y', SWAP)])  17.1 us
    all_to_all x1, blocking collectives, body(): parcel = lax.all_to_all(parcel, SEQ_GROUP, 0, 0, tiled=True)  15 us
    pallas_call x1, Pallas kernels, attend_back(): pl.pallas_call(attend_back_kernel, out_shape=(jax.ShapeDtypeStruct((rows,...  14.5 us
    all_to_all x1, waiting for transfers between devices, body(): input_parts = lax.all_to_all(input_parts, SEQ_GROUP, 0, 0, tiled=True)  12.4 us
  transfers between devices with their start and end apart: 27, of which 22 were waited for; matrix products, arithmetic and copies ran while one was open for 13% of the time, Pallas kernels for 6%

profile of v1, /device:TPU:0, one launch (start us, length us, event | category | flops | bytes accessed | tf_op | source)
XLA Modules:
  0.0 455.3 jit_solution(11205439849328668087)
XLA Ops:
  8.0 1.4 reshape.320
  9.5 1.1 reshape.321
  10.6 4.4 all-to-all-start.3
  16.0 5.3 %all-to-all-done.3 = bf16[4,24,1536]{2,1,0:T(8,128)(2,1)S(1)} async-done(((bf16[4,24,1536]{2,1,0:T(8,128)(2,1)}), bf16[4,24,1536]{2,1,0:T(8,128)(2,1)S(1)}, u32[]{:S(2)}, u32[]{:S(2)}) %all-to-all-start.3) | async-done | bytes 294944 | tf_op jit(solution)/shard_map/gather_ff_weights/all_to_all | solution.py:294
  21.3 15.0 %all_to_all.40 = bf16[8,24,640]{2,1,0:T(8,128)(2,1)S(1)} all-to-all(bf16[8,24,640]{2,1,0:T(8,128)(2,1)S(1)} %bitcast.161), channel_id=1, replica_groups=mesh['s'=2,'e'=1,'g'=4,'y'=2,'c'=2] {'s','g'}, dimensions={0} | all-to-all | bytes 491520 | tf_op jit(solution)/shard_map/gather_qkv_weights/all_to_all | solution.py:262
  36.3 1.0 broadcast_in_dim.67
  37.2 3.6 all-to-all-start.1
  41.6 8.9 %all-gather = bf16[32,24,640]{2,1,0:T(8,128)(2,1)S(1)} all-gather(bf16[8,24,640]{2,1,0:T(8,128)(2,1)S(1)} %all_to_all.40), channel_id=2, replica_groups=mesh['s'=2,'e'=1,'g'=4,'y'=2,'c'=2] {'e','y','c'}, dimensions={0}, use_global_device_ids=true | all-gather | bytes 1228800 | tf_op jit(solution)/shard_map/gather_qkv_weights/all_gather | solution.py:263
  51.3 11.7 %all-to-all-done.1 = bf16[8,64,768]{2,1,0:T(8,128)(2,1)S(1)} async-done(((bf16[8,64,768]{2,1,0:T(8,128)(2,1)}), bf16[8,64,768]{2,1,0:T(8,128)(2,1)S(1)}, u32[]{:S(2)}, u32[]{:S(2)}) %all-to-all-start.1) | async-done | bytes 786464 | tf_op jit(solution)/shard_map/gather_tokens/all_to_all | solution.py:224
  65.0 7.3 %collective-permute-done = bf16[512,384]{1,0:T(8,128)(2,1)S(1)} collective-permute-done((bf16[512,384]{1,0:T(8,128)(2,1)S(1)}, bf16[512,384]{1,0:T(8,128)(2,1)S(1)}, u32[]{:S(2)}, u32[]{:S(2)}) %collective-permute-start) | collective-permute-done | bytes 393248 | tf_op jit(solution)/shard_map/gather_kv/ppermute | solution.py:180
  73.7 1.4 copy.145
  75.8 1.3 pad_maximum_fusion.kv_ref
  77.2 11.0 %attend.1 = (bf16[512,192]{1,0:T(8,128)(2,1)}, f32[192,512]{1,0:T(8,128)}, f32[3,512]{1,0:T(4,128)}) custom-call(f32[3]{0:T(128)} %power_multiply_fusion.slopes_ref, bf16[512,192]{1,0:T(8,128)(2,1)} %slice.186.q_ref, bf16[2048,384]{1,0:T(8,128)(2,1)} %pad_maximum_fusion.kv_ref, f32[1,512]{1,0:T(1,128)} %get-tuple-element.61.pq_ref, f32[2048,1]{1,0:T(8,128)} %bitcast.156), custom_call_target="tpu_custom_call" | custom-call | flops 805306368 | bytes 1048576 | tf_op jit(solution)/shard_map/attention/attend/pallas_call | solution.py:92
  88.2 6.3 %all-to-all-start.2 = ((bf16[8,64,192]{2,1,0:T(8,128)(2,1)}), bf16[8,64,192]{2,1,0:T(8,128)(2,1)S(1)}, u32[]{:S(2)}, u32[]{:S(2)}) async-start(bf16[8,64,192]{2,1,0:T(8,128)(2,1)} %bitcast.167), calls=%async_computation.2 | async-start | bytes 524288 | tf_op jit(solution)/shard_map/return_attended/all_to_all | solution.py:343
  95.6 10.9 %all-to-all-done.2 = bf16[8,64,192]{2,1,0:T(8,128)(2,1)S(1)} async-done(((bf16[8,64,192]{2,1,0:T(8,128)(2,1)}), bf16[8,64,192]{2,1,0:T(8,128)(2,1)S(1)}, u32[]{:S(2)}, u32[]{:S(2)}) %all-to-all-start.2) | async-done | bytes 196640 | tf_op jit(solution)/shard_map/return_attended/all_to_all | solution.py:343
  107.0 1.8 fusion.54
  109.7 5.2 %collective-permute-done.2 = bf16[128,768]{1,0:T(8,128)(2,1)S(1)} collective-permute-done((bf16[128,768]{1,0:T(8,128)(2,1)S(1)}, bf16[128,768]{1,0:T(8,128)(2,1)S(1)}, u32[]{:S(2)}, u32[]{:S(2)}) %collective-permute-start.2) | collective-permute-done | bytes 196640 | tf_op jit(solution)/shard_map/gather_hidden/ppermute | solution.py:180
  115.3 1.4 collective-permute-done.3
  117.5 8.1 %all-gather.7.cloned.1.call-done = bf16[768,1536]{1,0:T(8,128)(2,1)} async-done(((bf16[96,1536]{1,0:T(8,128)(2,1)}), bf16[768,1536]{1,0:T(8,128)(2,1)}) %all-gather.7.cloned.1.call-update) | async-done | bytes 2359312 | tf_op jit(solution)/shard_map/gather_ff_weights/all_gather | solution.py:295
  125.6 3.3 convolution_add_fusion
  128.9 4.5 multiply_convert_fusion
  133.4 33.3 %all-gather.9.cloned.1.call-done = bf16[768,768]{1,0:T(8,128)(2,1)} async-done(((bf16[96,768]{1,0:T(8,128)(2,1)}), bf16[768,768]{1,0:T(8,128)(2,1)}) %all-gather.9.cloned.1.call-update) | async-done | bytes 1179664 | tf_op jit(solution)/shard_map/gather_ff_weights/all_gather | solution.py:298
  166.7 2.3 fusion.55
  169.0 1.1 copy-done.15
  173.0 2.2 slice_add_fusion.2
  175.2 1.7 slice.270
  176.9 1.5 collective-permute-start.5
  179.8 1.4 reshape.351
  181.2 2.9 collective-permute-done.5
  184.1 1.3 fusion.48
  188.0 1.5 collective-permute-start.6
  189.5 4.6 %collective-permute-done.6 = bf16[128,768]{1,0:T(8,128)(2,1)S(1)} collective-permute-done((bf16[128,768]{1,0:T(8,128)(2,1)S(1)}, bf16[128,768]{1,0:T(8,128)(2,1)S(1)}, u32[]{:S(2)}, u32[]{:S(2)}) %collective-permute-start.6) | collective-permute-done | bytes 196640 | tf_op jit(solution)/shard_map/gather_ff_grad/ppermute | solution.py:180
  194.3 1.7 collective-permute-done.7
  196.0 1.3 fusion.17
  197.8 1.4 fusion.44
  199.5 1.6 collective-permute-done.8
  201.2 1.5 collective-permute-start.9
  202.8 5.5 %collective-permute-done.9 = bf16[128,768]{1,0:T(8,128)(2,1)S(1)} collective-permute-done((bf16[128,768]{1,0:T(8,128)(2,1)S(1)}, bf16[128,768]{1,0:T(8,128)(2,1)S(1)}, u32[]{:S(2)}, u32[]{:S(2)}) %collective-permute-start.9) | collective-permute-done | bytes 196640 | tf_op jit(solution)/shard_map/sum_hidden_grad/ppermute | solution.py:190
  209.5 1.1 copy.134
  211.3 1.8 convolution_convert_fusion.1
  213.1 1.2 copy-done
  215.9 3.4 all-to-all-start.4
  219.6 4.7 %convolution_convert_fusion = bf16[768,1536]{1,0:T(8,128)(2,1)} fusion(bf16[256,768]{1,0:T(8,128)(2,1)S(1)} %copy-done.57, bf16[128,768]{1,0:T(8,128)(2,1)S(1)} %copy-done.24, bf16[128,768]{1,0:T(8,128)(2,1)S(1)} %copy-done.18, f32[512,768]{1,0:T(8,128)} %copy-done.8, f32[512,768]{1,0:T(8,128)} %copy-done.7), kind=kOutput, calls=%fused_computation | convolution fusion | flops 1213071360 | bytes 6291456 | tf_op jit(solution)/shard_map/ff_weight_grads/dot_general | solution.py:35
  224.4 3.6 all-to-all-done.4
  228.6 14.5 %attend_back.1 = (bf16[512,192]{1,0:T(8,128)(2,1)}, bf16[2048,384]{1,0:T(8,128)(2,1)}) custom-call(f32[3]{0:T(128)} %power_multiply_fusion.slopes_ref, bf16[512,192]{1,0:T(8,128)(2,1)} %slice.186.q_ref, bf16[2048,384]{1,0:T(8,128)(2,1)} %pad_maximum_fusion.kv_ref, f32[1,512]{1,0:T(1,128)} %get-tuple-element.61.pq_ref, f32[2048,1]{1,0:T(8,128)} %bitcast.157, ...), custom_call_target="tpu_custom_call" | custom-call | flops 2013265920 | bytes 1048576 | tf_op jit(solution)/shard_map/attention_back/attend_back/pallas_call | solution.py:147
  243.2 1.3 slice.164
  244.6 2.3 collective-permute-done.10
  247.1 1.6 collective-permute-start.11
  250.2 2.1 convert_reduce_fusion
  255.2 3.1 collective-permute-done.11
  258.4 2.9 convolution_convert_fusion.3
  261.4 3.7 all-to-all-start.5
  266.2 2.1 convolution_bitcast_fusion
  268.2 1.9 copy.130
  270.3 1.9 collective-permute-done.12
  273.1 12.4 %all-to-all-done.5 = bf16[8,64,768]{2,1,0:T(8,128)(2,1)S(1)} async-done(((bf16[8,64,768]{2,1,0:T(8,128)(2,1)}), bf16[8,64,768]{2,1,0:T(8,128)(2,1)S(1)}, u32[]{:S(2)}, u32[]{:S(2)}) %all-to-all-start.5) | async-done | bytes 786464 | tf_op jit(solution)/shard_map/input_grad/all_to_all | solution.py:441
  285.5 4.8 %all-to-all-start.6 = ((bf16[16,24,640]{2,1,0:T(8,128)(2,1)}), bf16[16,24,640]{2,1,0:T(8,128)(2,1)S(1)}, u32[]{:S(2)}, u32[]{:S(2)}) async-start(bf16[16,24,640]{2,1,0:T(8,128)(2,1)} %fusion.15), calls=%async_computation.6 | async-start | bytes 983040 | tf_op jit(solution)/shard_map/qkv_weight_grad/all_to_all | solution.py:478
  291.0 20.3 %reduce-scatter.11.cloned.1.call-done = bf16[96,768]{1,0:T(8,128)(2,1)} async-done(((bf16[768,768]{1,0:T(8,128)(2,1)}), bf16[96,768]{1,0:T(8,128)(2,1)}) %reduce-scatter.11.cloned.1.call-update) | async-done | bytes 147472 | tf_op jit(solution)/shard_map/ff_weight_grads/reduce_scatter | solution.py:386
  311.3 1.6 convert_element_type.306
  317.8 65.4 %reduce-scatter.9.cloned.1.call-done = bf16[96,1536]{1,0:T(8,128)(2,1)} async-done(((bf16[768,1536]{1,0:T(8,128)(2,1)}), bf16[96,1536]{1,0:T(8,128)(2,1)}) %reduce-scatter.9.cloned.1.call-update) | async-done | bytes 294928 | tf_op jit(solution)/shard_map/ff_weight_grads/reduce_scatter | solution.py:389
  383.2 3.5 all-to-all-start.7
  387.3 57.4 %reduce-scatter.7.cloned.1.call-done = bf16[24,768]{1,0:T(8,128)(2,1)} async-done(((bf16[192,768]{1,0:T(8,128)(2,1)}), bf16[24,768]{1,0:T(8,128)(2,1)}) %reduce-scatter.7.cloned.1.call-update) | async-done | bytes 36880 | tf_op jit(solution)/shard_map/attn_weight_grad/reduce_scatter | solution.py:425
  444.7 1.4 convert_element_type.299
  446.9 1.6 reshape.354
  (275 shorter events, 36.8 us)
Async XLA Ops:
  7.2 7.8 %copy-start.60 = (bf16[2,24]{1,0:T(2,128)(2,1)S(1)}, bf16[2,24]{1,0:T(2,128)(2,1)}, u32[]{:S(2)}) copy-start(bf16[2,24]{1,0:T(2,128)(2,1)} %param.18) | copy-start | bytes 292
  7.2 7.8 %copy-start.46 = (bf16[24]{0:T(256)(128)(2,1)S(1)}, bf16[24]{0:T(256)(128)(2,1)}, u32[]{:S(2)}) copy-start(bf16[24]{0:T(256)(128)(2,1)} %param.20) | copy-start | bytes 148
  7.2 7.8 %copy-start.47 = (bf16[24]{0:T(256)(128)(2,1)S(1)}, bf16[24]{0:T(256)(128)(2,1)}, u32[]{:S(2)}) copy-start(bf16[24]{0:T(256)(128)(2,1)} %param.21) | copy-start | bytes 148
  7.2 7.8 %copy-start.48 = (bf16[24]{0:T(256)(128)(2,1)S(1)}, bf16[24]{0:T(256)(128)(2,1)}, u32[]{:S(2)}) copy-start(bf16[24]{0:T(256)(128)(2,1)} %param.22) | copy-start | bytes 148
  7.2 7.8 %copy-start.52 = (bf16[192]{0:T(256)(128)(2,1)S(1)}, bf16[192]{0:T(256)(128)(2,1)}, u32[]{:S(2)}) copy-start(bf16[192]{0:T(256)(128)(2,1)} %param.24) | copy-start | bytes 1156
  7.2 7.8 %copy-start.49 = (bf16[24]{0:T(256)(128)(2,1)S(1)}, bf16[24]{0:T(256)(128)(2,1)}, u32[]{:S(2)}) copy-start(bf16[24]{0:T(256)(128)(2,1)} %param.26) | copy-start | bytes 148
  7.2 7.8 %copy-start.50 = (bf16[24]{0:T(256)(128)(2,1)S(1)}, bf16[24]{0:T(256)(128)(2,1)}, u32[]{:S(2)}) copy-start(bf16[24]{0:T(256)(128)(2,1)} %param.27) | copy-start | bytes 148
  7.3 7.8 %copy-start.51 = (bf16[24]{0:T(256)(128)(2,1)S(1)}, bf16[24]{0:T(256)(128)(2,1)}, u32[]{:S(2)}) copy-start(bf16[24]{0:T(256)(128)(2,1)} %param.28) | copy-start | bytes 148
  7.3 7.9 %copy-start.53 = (s32[2,256]{1,0:T(2,128)S(1)}, s32[2,256]{1,0:T(2,128)}, u32[]{:S(2)}) copy-start(s32[2,256]{1,0:T(2,128)} %param.16) | copy-start | bytes 6148
  7.3 8.2 %copy-start.28 = (bf16[24,2304]{1,0:T(8,128)(2,1)S(1)}, bf16[24,2304]{1,0:T(8,128)(2,1)}, u32[]{:S(2)}) copy-start(bf16[24,2304]{1,0:T(8,128)(2,1)} %param.17) | copy-start | bytes 331780
  7.3 99.7 %all-gather.5.cloned.1.call-start = ((), (), s32[]{:S(2)}) async-start(), calls=%async_computation.12 | async-start | bytes 1216512 | tf_op jit(solution)/shard_map/gather_ff_weights/all_gather | solution.py:299
  10.6 25.7 %copy-start.16 = (bf16[2,64,768]{2,1,0:T(8,128)(2,1)S(1)}, bf16[2,64,768]{2,1,0:T(8,128)(2,1)}, u32[]{:S(2)}) copy-start(bf16[2,64,768]{2,1,0:T(8,128)(2,1)} %param.15) | copy-start | bytes 589828
  10.6 10.8 %all-to-all-start.3 = ((bf16[4,24,1536]{2,1,0:T(8,128)(2,1)}), bf16[4,24,1536]{2,1,0:T(8,128)(2,1)S(1)}, u32[]{:S(2)}, u32[]{:S(2)}) async-start(bf16[4,24,1536]{2,1,0:T(8,128)(2,1)} %reshape.321), calls=%async_computation.3 | async-start | bytes 589824 | tf_op jit(solution)/shard_map/gather_ff_weights/all_to_all | solution.py:294
  21.3 19.6 %copy-start.11 = (bf16[4,24,1536]{2,1,0:T(8,128)(2,1)}, bf16[4,24,1536]{2,1,0:T(8,128)(2,1)S(1)}, u32[]{:S(2)}) copy-start(bf16[4,24,1536]{2,1,0:T(8,128)(2,1)S(1)} %all-to-all-done.3) | copy-start | bytes 884740
  37.2 25.8 %all-to-all-start.1 = ((bf16[8,64,768]{2,1,0:T(8,128)(2,1)}), bf16[8,64,768]{2,1,0:T(8,128)(2,1)S(1)}, u32[]{:S(2)}, u32[]{:S(2)}) async-start(bf16[8,64,768]{2,1,0:T(8,128)(2,1)} %bitcast.6), calls=%async_computation.1 | async-start | bytes 1572864 | tf_op jit(solution)/shard_map/gather_tokens/all_to_all | solution.py:224
  40.8 84.7 %all-gather.7.cloned.1.call-start = ((), (), s32[]{:S(2)}) async-start(), calls=%async_computation.13 | async-start | bytes 2654208 | tf_op jit(solution)/shard_map/gather_ff_weights/all_gather | solution.py:295
  51.1 11.9 %copy-start.14 = (bf16[2,1,4,2,2,24,576]{6,5,4,3,2,0,1:T(8,128)(2,1)}, bf16[2,1,4,2,2,24,576]{6,5,4,3,2,0,1:T(8,128)(2,1)S(1)}, u32[]{:S(2)}) copy-start(bf16[2,1,4,2,2,24,576]{6,5,4,3,2,0,1:T(8,128)(2,1)S(1)} %copy.113) | copy-start | bytes 2654212
  64.1 8.2 %collective-permute-start = (bf16[512,384]{1,0:T(8,128)(2,1)S(1)}, bf16[512,384]{1,0:T(8,128)(2,1)S(1)}, u32[]{:S(2)}, u32[]{:S(2)}) collective-permute-start(bf16[512,384]{1,0:T(8,128)(2,1)S(1)} %slice.187), channel_id=1, source_target_pairs={{0,2},{2,0},{1,3},{3,1},{4,6},{6,4},{5,7},{7,5},{8,10},{10,8},{9,1... | collective-permute-start | bytes 1179656 | tf_op jit(solution)/shard_map/gather_kv/ppermute | solution.py:180
  72.4 3.5 collective-permute-start.1
  88.2 18.3 %all-to-all-start.2 = ((bf16[8,64,192]{2,1,0:T(8,128)(2,1)}), bf16[8,64,192]{2,1,0:T(8,128)(2,1)S(1)}, u32[]{:S(2)}, u32[]{:S(2)}) async-start(bf16[8,64,192]{2,1,0:T(8,128)(2,1)} %bitcast.167), calls=%async_computation.2 | async-start | bytes 524288 | tf_op jit(solution)/shard_map/return_attended/all_to_all | solution.py:343
  94.5 72.2 %all-gather.9.cloned.1.call-start = ((), (), s32[]{:S(2)}) async-start(), calls=%async_computation.14 | async-start | bytes 1327104 | tf_op jit(solution)/shard_map/gather_ff_weights/all_gather | solution.py:298
  107.0 8.0 %copy-start.3 = (bf16[128,768]{1,0:T(8,128)(2,1)}, bf16[128,768]{1,0:T(8,128)(2,1)S(1)}, u32[]{:S(2)}) copy-start(bf16[128,768]{1,0:T(8,128)(2,1)S(1)} %reshape.319) | copy-start | bytes 589828
  108.8 8.0 %copy-start.40 = (f32[128]{0:T(128)}, f32[128]{0:T(128)S(1)}, u32[]{:S(2)}) copy-start(f32[128]{0:T(128)S(1)} %broadcast_multiply_fusion.1) | copy-start | bytes 1540
  109.0 7.8 %copy-start.44 = (f32[128]{0:T(128)}, f32[128]{0:T(128)S(1)}, u32[]{:S(2)}) copy-start(f32[128]{0:T(128)S(1)} %multiply_reduce_fusion.3) | copy-start | bytes 1540
  109.0 7.7 %copy-start.42 = (f32[128]{0:T(128)}, f32[128]{0:T(128)S(1)}, u32[]{:S(2)}) copy-start(f32[128]{0:T(128)S(1)} %fusion.34) | copy-start | bytes 1540
  109.1 7.6 %copy-start.17 = (bf16[128,768]{1,0:T(8,128)(2,1)}, bf16[128,768]{1,0:T(8,128)(2,1)S(1)}, u32[]{:S(2)}) copy-start(bf16[128,768]{1,0:T(8,128)(2,1)S(1)} %fusion.26) | copy-start | bytes 589828
  109.2 5.7 %collective-permute-start.2 = (bf16[128,768]{1,0:T(8,128)(2,1)S(1)}, bf16[128,768]{1,0:T(8,128)(2,1)S(1)}, u32[]{:S(2)}, u32[]{:S(2)}) collective-permute-start(bf16[128,768]{1,0:T(8,128)(2,1)S(1)} %fusion.26), channel_id=1, source_target_pairs={{0,2},{2,0},{1,3},{3,1},{4,6},{6,4},{5,7},{7,5},{8,10},{10,8},{9,1... | collective-permute-start | bytes 589832 | tf_op jit(solution)/shard_map/gather_hidden/ppermute | solution.py:180
  109.5 180.8 %reduce-scatter.5.cloned.1.call-start = ((), (), s32[]{:S(2)}) async-start(), calls=%async_computation.15 | async-start | bytes 1474560 | tf_op jit(solution)/shard_map/attn_weight_grad/reduce_scatter | solution.py:424
  114.9 1.8 collective-permute-start.3
  170.9 2.1 collective-permute-start.4
  172.4 6.0 %copy-start.35 = (f32[1,2,2,2,4,24]{5,4,3,2,1,0:T(4,128)S(1)}, f32[1,2,2,2,4,24]{5,4,3,2,1,0:T(4,128)}, u32[]{:S(2)}) copy-start(f32[1,2,2,2,4,24]{5,4,3,2,1,0:T(4,128)} %get-tuple-element.45) | copy-start | bytes 9220
  172.4 6.0 %copy-start.36 = (f32[1,2,2,2,4,24]{5,4,3,2,1,0:T(4,128)S(1)}, f32[1,2,2,2,4,24]{5,4,3,2,1,0:T(4,128)}, u32[]{:S(2)}) copy-start(f32[1,2,2,2,4,24]{5,4,3,2,1,0:T(4,128)} %get-tuple-element.50) | copy-start | bytes 9220
  176.9 7.3 %collective-permute-start.5 = (bf16[128,768]{1,0:T(8,128)(2,1)}, bf16[128,768]{1,0:T(8,128)(2,1)}, u32[]{:S(2)}, u32[]{:S(2)}) collective-permute-start(bf16[128,768]{1,0:T(8,128)(2,1)} %slice.270), channel_id=1, source_target_pairs={{0,2},{2,0},{1,3},{3,1},{4,6},{6,4},{5,7},{7,5},{8,10},{10,8},{9,1... | collective-permute-start | bytes 589832 | tf_op jit(solution)/shard_map/sum_ff/ppermute | solution.py:190
  181.2 5.2 %copy-start.39 = (f32[768]{0:T(1024)S(1)}, f32[768]{0:T(1024)}, u32[]{:S(2)}) copy-start(f32[768]{0:T(1024)} %reshape.351) | copy-start | bytes 9220
  185.6 10.3 %copy-start.10 = (f32[512,768]{1,0:T(8,128)S(1)}, f32[512,768]{1,0:T(8,128)}, u32[]{:S(2)}) copy-start(f32[512,768]{1,0:T(8,128)} %get-tuple-element.41) | copy-start | bytes 4718596
  185.7 10.3 %copy-start.55 = (bf16[768,768]{1,0:T(8,128)(2,1)S(1)}, bf16[768,768]{1,0:T(8,128)(2,1)}, u32[]{:S(2)}) copy-start(bf16[768,768]{1,0:T(8,128)(2,1)} %all-gather.9.cloned.1.call-done) | copy-start | bytes 3538948
  188.0 9.3 %copy-start.19 = (bf16[128,768]{1,0:T(8,128)(2,1)}, bf16[128,768]{1,0:T(8,128)(2,1)S(1)}, u32[]{:S(2)}) copy-start(bf16[128,768]{1,0:T(8,128)(2,1)S(1)} %get-tuple-element.30) | copy-start | bytes 589828
  188.0 6.1 %collective-permute-start.6 = (bf16[128,768]{1,0:T(8,128)(2,1)S(1)}, bf16[128,768]{1,0:T(8,128)(2,1)S(1)}, u32[]{:S(2)}, u32[]{:S(2)}) collective-permute-start(bf16[128,768]{1,0:T(8,128)(2,1)S(1)} %get-tuple-element.30), channel_id=1, source_target_pairs={{0,2},{2,0},{1,3},{3,1},{4,6},{6,4},{5,7},{7,5},{8,10},{10,8},{9,1... | collective-permute-start | bytes 589832 | tf_op jit(solution)/shard_map/gather_ff_grad/ppermute | solution.py:180
  194.2 1.8 collective-permute-start.7
  199.3 9.0 %copy-start.41 = (f32[128]{0:T(128)S(1)}, f32[128]{0:T(128)}, u32[]{:S(2)}) copy-start(f32[128]{0:T(128)} %copy-done.40) | copy-start | bytes 1540
  199.3 9.0 %copy-start.43 = (f32[128]{0:T(128)S(1)}, f32[128]{0:T(128)}, u32[]{:S(2)}) copy-start(f32[128]{0:T(128)} %copy-done.42) | copy-start | bytes 1540
  199.3 1.8 collective-permute-start.8
  201.2 7.4 %copy-start.45 = (f32[128]{0:T(128)S(1)}, f32[128]{0:T(128)}, u32[]{:S(2)}) copy-start(f32[128]{0:T(128)} %copy-done.44) | copy-start | bytes 1540
  201.2 7.7 %copy-start.4 = (bf16[128,768]{1,0:T(8,128)(2,1)S(1)}, bf16[128,768]{1,0:T(8,128)(2,1)}, u32[]{:S(2)}) copy-start(bf16[128,768]{1,0:T(8,128)(2,1)} %copy-done.3) | copy-start | bytes 589828
  201.2 7.0 %collective-permute-start.9 = (bf16[128,768]{1,0:T(8,128)(2,1)S(1)}, bf16[128,768]{1,0:T(8,128)(2,1)S(1)}, u32[]{:S(2)}, u32[]{:S(2)}) collective-permute-start(bf16[128,768]{1,0:T(8,128)(2,1)S(1)} %slice.269), channel_id=1, source_target_pairs={{0,2},{2,0},{1,3},{3,1},{4,6},{6,4},{5,7},{7,5},{8,10},{10,8},{9,1... | collective-permute-start | bytes 589832 | tf_op jit(solution)/shard_map/sum_hidden_grad/ppermute | solution.py:190
  210.6 100.7 %reduce-scatter.11.cloned.1.call-start = ((), (), s32[]{:S(2)}) async-start(), calls=%async_computation.18 | async-start | bytes 1327104 | tf_op jit(solution)/shard_map/ff_weight_grads/reduce_scatter | solution.py:386
  214.4 5.2 %copy-start.18 = (bf16[128,768]{1,0:T(8,128)(2,1)S(1)}, bf16[128,768]{1,0:T(8,128)(2,1)}, u32[]{:S(2)}) copy-start(bf16[128,768]{1,0:T(8,128)(2,1)} %copy-done.17) | copy-start | bytes 589828
  214.4 5.2 %copy-start.24 = (bf16[128,768]{1,0:T(8,128)(2,1)S(1)}, bf16[128,768]{1,0:T(8,128)(2,1)}, u32[]{:S(2)}) copy-start(bf16[128,768]{1,0:T(8,128)(2,1)} %copy-done.23) | copy-start | bytes 589828
  214.4 5.2 %copy-start.57 = (bf16[256,768]{1,0:T(8,128)(2,1)S(1)}, bf16[256,768]{1,0:T(8,128)(2,1)}, u32[]{:S(2)}) copy-start(bf16[256,768]{1,0:T(8,128)(2,1)} %copy-done.56) | copy-start | bytes 1179652
  215.9 12.0 %all-to-all-start.4 = ((bf16[8,64,192]{2,1,0:T(8,128)(2,1)}), bf16[8,64,192]{2,1,0:T(8,128)(2,1)S(1)}, u32[]{:S(2)}, u32[]{:S(2)}) async-start(bf16[8,64,192]{2,1,0:T(8,128)(2,1)} %bitcast.34), calls=%async_computation.4 | async-start | bytes 524288 | tf_op jit(solution)/shard_map/send_out_grad/all_to_all | solution.py:407
  219.3 163.9 %reduce-scatter.9.cloned.1.call-start = ((), (), s32[]{:S(2)}) async-start(), calls=%async_computation.17 | async-start | bytes 2654208 | tf_op jit(solution)/shard_map/ff_weight_grads/reduce_scatter | solution.py:389
  244.5 5.0 %copy-start.37 = (f32[768]{0:T(1024)S(1)}, f32[768]{0:T(1024)}, u32[]{:S(2)}) copy-start(f32[768]{0:T(1024)} %get-tuple-element.26) | copy-start | bytes 9220
  244.5 2.4 collective-permute-start.10
  247.1 11.2 %collective-permute-start.11 = (bf16[512,384]{1,0:T(8,128)(2,1)S(1)}, bf16[512,384]{1,0:T(8,128)(2,1)S(1)}, u32[]{:S(2)}, u32[]{:S(2)}) collective-permute-start(bf16[512,384]{1,0:T(8,128)(2,1)S(1)} %slice.266), channel_id=1, source_target_pairs={{0,2},{2,0},{1,3},{3,1},{4,6},{6,4},{5,7},{7,5},{8,10},{10,8},{9,1... | collective-permute-start | bytes 1179656 | tf_op jit(solution)/shard_map/sum_kv_grads/ppermute | solution.py:190
  252.3 6.1 %copy-start.12 = (bf16[512,192]{1,0:T(8,128)(2,1)S(1)}, bf16[512,192]{1,0:T(8,128)(2,1)}, u32[]{:S(2)}) copy-start(bf16[512,192]{1,0:T(8,128)(2,1)} %get-tuple-element.22) | copy-start | bytes 589828
  261.4 4.5 copy-start.32
  261.4 4.5 copy-start.33
  261.4 4.8 %copy-start.2 = (bf16[8,64,768]{2,1,0:T(8,128)(2,1)S(1)}, bf16[8,64,768]{2,1,0:T(8,128)(2,1)}, u32[]{:S(2)}) copy-start(bf16[8,64,768]{2,1,0:T(8,128)(2,1)} %copy-done.1) | copy-start | bytes 2359300
  261.4 4.8 %copy-start.13 = (bf16[512,192]{1,0:T(8,128)(2,1)S(1)}, bf16[512,192]{1,0:T(8,128)(2,1)}, u32[]{:S(2)}) copy-start(bf16[512,192]{1,0:T(8,128)(2,1)} %get-tuple-element.22) | copy-start | bytes 589828
  261.4 24.1 %all-to-all-start.5 = ((bf16[8,64,768]{2,1,0:T(8,128)(2,1)}), bf16[8,64,768]{2,1,0:T(8,128)(2,1)S(1)}, u32[]{:S(2)}, u32[]{:S(2)}) async-start(bf16[8,64,768]{2,1,0:T(8,128)(2,1)} %bitcast.162), calls=%async_computation.5 | async-start | bytes 1572864 | tf_op jit(solution)/shard_map/input_grad/all_to_all | solution.py:441
  270.2 1.9 collective-permute-start.12
  285.5 28.4 %all-to-all-start.6 = ((bf16[16,24,640]{2,1,0:T(8,128)(2,1)}), bf16[16,24,640]{2,1,0:T(8,128)(2,1)S(1)}, u32[]{:S(2)}, u32[]{:S(2)}) async-start(bf16[16,24,640]{2,1,0:T(8,128)(2,1)} %fusion.15), calls=%async_computation.6 | async-start | bytes 983040 | tf_op jit(solution)/shard_map/qkv_weight_grad/all_to_all | solution.py:478
  290.2 154.4 %reduce-scatter.7.cloned.1.call-start = ((), (), s32[]{:S(2)}) async-start(), calls=%async_computation.16 | async-start | bytes 331776 | tf_op jit(solution)/shard_map/attn_weight_grad/reduce_scatter | solution.py:425
  383.2 62.8 %all-to-all-start.7 = ((bf16[4,24,1536]{2,1,0:T(8,128)(2,1)}), bf16[4,24,1536]{2,1,0:T(8,128)(2,1)S(1)}, u32[]{:S(2)}, u32[]{:S(2)}) async-start(bf16[4,24,1536]{2,1,0:T(8,128)(2,1)} %bitcast.165), calls=%async_computation.10 | async-start | bytes 589824 | tf_op jit(solution)/shard_map/ff_weight_grads/all_to_all | solution.py:392
  (24 other events, 62.0 us)
Sparse Core Ops, SparseCore 0:
  11.0 59.6 all-gather.4
  73.5 52.0 all-gather.6
  127.8 38.8 all-gather.8
  210.7 24.4 reduce-scatter.4
  238.8 72.4 reduce-scatter.10
  315.1 68.1 reduce-scatter.8
  386.9 57.7 reduce-scatter.6

commit v2 on v1

v2 whole, which is shorter than its diff:
```python
import functools

import jax
import jax.numpy as jnp
from jax import lax
from jax.experimental import pallas as pl
from jax.experimental.pallas import tpu as pltpu
from jax.sharding import Mesh
from jax.sharding import PartitionSpec as P

HEADS = 12
HEAD_DIM = 64
GROUPS = 4
GROUP_HEADS = HEADS // GROUPS
GROUP_WIDTH = GROUP_HEADS * HEAD_DIM
EPSILON = 1e-12
SCORE_SCALE = 0.125
LOG2E = 1.4426950408889634
LOWEST = -1e30
KEY_BLOCK = 512
FF_TILE = 256
SEQ_GROUP = ("s", "r", "x")
CHUNKS = ("e", "y", "c")
RING = ("s", "e", "r")
PLANE = ("x", "y")
SEQ_AXIS = ("s", "e", "r", "x")
EVERY = ("s", "e", "r", "x", "y", "c")
SWAP = ((0, 1), (1, 0))
BF16 = jnp.bfloat16
F32 = jnp.float32
VMEM_BYTES = 60 * 2**20


def nt(a, b):
    return lax.dot_general(a, b, (((1,), (1,)), ((), ())), preferred_element_type=F32)


def tn(a, b):
    return lax.dot_general(a, b, (((0,), (0,)), ((), ())), preferred_element_type=F32)


def nn(a, b):
    return lax.dot_general(a, b, (((1,), (0,)), ((), ())), preferred_element_type=F32)


def head_cols(head, base=0):
    return slice(base + head * HEAD_DIM, base + (head + 1) * HEAD_DIM)


def log2_scores(keys, queries, slope, key_pos, query_pos):
    products = nt(keys, queries)
    distances = jnp.abs(key_pos * slope - query_pos * slope)
    return products * (SCORE_SCALE * LOG2E) - distances


def column(row):
    return jnp.broadcast_to(row, (8, row.shape[1])).T[:, :1]


def key_blocks(kv_refs):
    start = 0
    for piece in kv_refs:
        yield piece, start
        start += piece.shape[0]


def turn_positions(pk_ref, column_ref):
    def turn(block, carry):
        at = pl.ds(pl.multiple_of(block * KEY_BLOCK, KEY_BLOCK), KEY_BLOCK)
        column_ref[at, :] = column(pk_ref[pl.ds(block, 1), :])
        return carry

    lax.fori_loop(0, pk_ref.shape[0], turn, 0)


def attend_kernel(count, first, last, slopes_ref, q_ref, pq_ref, pk_ref, *refs):
    kv_refs, refs = refs[:count], refs[count:]
    if not first:
        (sum_in_ref, stat_in_ref), refs = refs[:2], refs[2:]
    sum_ref, stat_ref = refs[:2]
    column_ref = refs[-1]
    rows = q_ref.shape[0]
    query_pos = pq_ref[...]
    turn_positions(pk_ref, column_ref)
    for head in range(GROUP_HEADS):
        slope = slopes_ref[head]
        queries = q_ref[:, head_cols(head)]
        if first:
            carry = (
                jnp.full((1, rows), LOWEST, F32),
                jnp.zeros((1, rows), F32),
                jnp.zeros((HEAD_DIM, rows), F32),
            )
        else:
            carry = (
                stat_in_ref[head : head + 1, :],
                stat_in_ref[GROUP_HEADS + head : GROUP_HEADS + head + 1, :],
                sum_in_ref[head_cols(head), :],
            )
        for kv_ref, start in key_blocks(kv_refs):

            def visit(block, carry, kv_ref=kv_ref, start=start):
                top, total, summed = carry
                at = pl.ds(pl.multiple_of(block * KEY_BLOCK, KEY_BLOCK), KEY_BLOCK)
                pos_at = pl.ds(
                    pl.multiple_of(start + block * KEY_BLOCK, KEY_BLOCK), KEY_BLOCK
                )
                keys = kv_ref[at, head_cols(head)]
                values = kv_ref[at, head_cols(head, GROUP_WIDTH)]
                scores = log2_scores(keys, queries, slope, column_ref[pos_at, :], query_pos)
                new_top = jnp.maximum(top, jnp.max(scores, axis=0, keepdims=True))
                weights = jnp.exp2(scores - new_top)
                shrink = jnp.exp2(top - new_top)
                total = total * shrink + jnp.sum(weights, axis=0, keepdims=True)
                summed = summed * shrink + tn(values, weights.astype(BF16))
                return new_top, total, summed

            carry = lax.fori_loop(0, kv_ref.shape[0] // KEY_BLOCK, visit, carry)
        top, total, summed = carry
        if last:
            attended = summed / total
            sum_ref[head_cols(head), :] = attended
            refs[2][:, head_cols(head)] = attended.T.astype(BF16)
            stat_ref[head : head + 1, :] = top + jnp.log2(total)
        else:
            sum_ref[head_cols(head), :] = summed
            stat_ref[head : head + 1, :] = top
            stat_ref[GROUP_HEADS + head : GROUP_HEADS + head + 1, :] = total


def attend(slopes, queries, query_pos, key_pos, key_values, state, last):
    rows, length = queries.shape[0], key_pos.size
    vmem = pl.BlockSpec(memory_space=pltpu.VMEM)
    count = len(key_values)
    first = state is None
    state = () if first else state
    outs = [
        jax.ShapeDtypeStruct((GROUP_WIDTH, rows), F32),
        jax.ShapeDtypeStruct((GROUP_HEADS * (1 if last else 2), rows), F32),
    ]
    if last:
        outs.append(jax.ShapeDtypeStruct((rows, GROUP_WIDTH), BF16))
    return pl.pallas_call(
        functools.partial(attend_kernel, count, first, last),
        out_shape=tuple(outs),
        in_specs=[pl.BlockSpec(memory_space=pltpu.SMEM)] + [vmem] * (3 + count + len(state)),
        out_specs=(vmem,) * len(outs),
        scratch_shapes=[pltpu.VMEM((length, 1), F32)],
        compiler_params=pltpu.CompilerParams(vmem_limit_bytes=VMEM_BYTES),
        cost_estimate=pl.CostEstimate(
            flops=64 * rows * length * GROUP_WIDTH,
            bytes_accessed=rows * length,
            transcendentals=rows * length * GROUP_HEADS,
        ),
        name="attend",
    )(slopes, queries, query_pos, key_pos, *key_values, *state)


def attend_back_kernel(
    count, first, last, slopes_ref, q_ref, pq_ref, pk_ref, do_ref, out_ref, lse_ref, _, *refs
):
    kv_refs, refs = refs[:count], refs[count:]
    if not first:
        dq_in_ref, refs = refs[0], refs[1:]
    dq_ref, dkv_refs, column_ref = refs[0], refs[1 : count + 1], refs[-1]
    rows = q_ref.shape[0]
    query_pos = pq_ref[...]
    turn_positions(pk_ref, column_ref)
    for head in range(GROUP_HEADS):
        slope = slopes_ref[head]
        queries = q_ref[:, head_cols(head)]
        out_grads = do_ref[:, head_cols(head)]
        log_sum = lse_ref[head : head + 1, :]
        delta = jnp.sum(
            out_grads.astype(F32).T * out_ref[head_cols(head), :], axis=0, keepdims=True
        )
        if first:
            query_grads = jnp.zeros((HEAD_DIM, rows), F32)
        else:
            query_grads = dq_in_ref[head_cols(head), :]
        for (kv_ref, start), dkv_ref in zip(key_blocks(kv_refs), dkv_refs):

            def visit(block, query_grads, kv_ref=kv_ref, start=start, dkv_ref=dkv_ref):
                at = pl.ds(pl.multiple_of(block * KEY_BLOCK, KEY_BLOCK), KEY_BLOCK)
                pos_at = pl.ds(
                    pl.multiple_of(start + block * KEY_BLOCK, KEY_BLOCK), KEY_BLOCK
                )
                keys = kv_ref[at, head_cols(head)]
                values = kv_ref[at, head_cols(head, GROUP_WIDTH)]
                scores = log2_scores(keys, queries, slope, column_ref[pos_at, :], query_pos)
                probs = jnp.exp2(scores - log_sum)
                prob_grads = nt(values, out_grads)
                score_grads = (probs * (prob_grads - delta)).astype(BF16)
                dkv_ref[at, head_cols(head, GROUP_WIDTH)] = nn(
                    probs.astype(BF16), out_grads
                ).astype(BF16)
                dkv_ref[at, head_cols(head)] = (nn(score_grads, queries) * SCORE_SCALE).astype(
                    BF16
                )
                return query_grads + tn(keys, score_grads)

            query_grads = lax.fori_loop(0, kv_ref.shape[0] // KEY_BLOCK, visit, query_grads)
        if last:
            dq_ref[:, head_cols(head)] = (query_grads * SCORE_SCALE).T.astype(BF16)
        else:
            dq_ref[head_cols(head), :] = query_grads


def attend_back(
    slopes,
    queries,
    query_pos,
    key_pos,
    out_grads,
    attended,
    log_sums,
    key_values,
    state,
    last,
    earlier,
):
    rows, length = queries.shape[0], key_pos.size
    vmem = pl.BlockSpec(memory_space=pltpu.VMEM)
    count = len(key_values)
    first = state is None
    state = () if first else (state,)
    query_out = (
        jax.ShapeDtypeStruct((rows, GROUP_WIDTH), BF16)
        if last
        else jax.ShapeDtypeStruct((GROUP_WIDTH, rows), F32)
    )
    return pl.pallas_call(
        functools.partial(attend_back_kernel, count, first, last),
        out_shape=(query_out,)
        + tuple(jax.ShapeDtypeStruct(piece.shape, BF16) for piece in key_values),
        in_specs=[pl.BlockSpec(memory_space=pltpu.SMEM)]
        + [vmem] * 6
        + [pl.BlockSpec(memory_space=pl.ANY)]
        + [vmem] * (count + len(state)),
        out_specs=(vmem,) * (1 + count),
        scratch_shapes=[pltpu.VMEM((length, 1), F32)],
        compiler_params=pltpu.CompilerParams(vmem_limit_bytes=VMEM_BYTES),
        cost_estimate=pl.CostEstimate(
            flops=84 * rows * length * GROUP_WIDTH,
            bytes_accessed=rows * length,
            transcendentals=rows * length * GROUP_HEADS,
        ),
        name="attend_back",
    )(
        slopes,
        queries,
        query_pos,
        key_pos,
        out_grads,
        attended,
        log_sums,
        earlier,
        *key_values,
        *state,
    )


def assemble(core_ref, own_ref, swap_ref, columns, target, sems):
    core = core_ref[0]
    copies = []
    for which, (piece, half) in enumerate(((own_ref, core), (swap_ref, 1 - core))):
        copy = pltpu.make_async_copy(piece.at[:, columns], target.at[half], sems.at[which])
        copy.start()
        copies.append(copy)
    return copies


def first_norm_kernel(
    columns,
    core_ref,
    mixed_ref,
    rows_ref,
    vec_ref,
    own_ref,
    swap_ref,
    low_ref,
    hidden_ref,
    normal_ref,
    scale_ref,
    weight_ref,
    sems,
):
    for copy in assemble(core_ref, own_ref, swap_ref, columns, weight_ref, sems):
        copy.wait()
    mixed = mixed_ref[...]
    lin = jnp.concatenate([nn(mixed, weight_ref[0]), nn(mixed, weight_ref[1])], axis=1)
    total = rows_ref[...].astype(F32) + (lin + vec_ref[2:3, :])
    normal, scale = normalised(total)
    hidden = normal * vec_ref[3:4, :] + vec_ref[4:5, :]
    low_ref[...] = hidden.astype(BF16)
    hidden_ref[...] = hidden
    normal_ref[...] = normal
    scale_ref[...] = scale


def normalised(values):
    centred = values - jnp.mean(values, axis=1, keepdims=True)
    variance = jnp.mean(centred * centred, axis=1, keepdims=True)
    scale = lax.rsqrt(variance + EPSILON)
    return centred * scale, scale


def norm_back(grads, normal, scale, gain):
    scaled = grads * gain
    return (
        scaled
        - jnp.mean(scaled, axis=1, keepdims=True)
        - normal * jnp.mean(scaled * normal, axis=1, keepdims=True)
    ) * scale


def column_sum(values):
    return jnp.sum(values, axis=0, keepdims=True)


def first_norm(core, mixed, rows, vectors, own, swap, columns):
    tokens, width = mixed.shape
    vmem = pl.BlockSpec(memory_space=pltpu.VMEM)
    half = own.shape[1]
    return pl.pallas_call(
        functools.partial(first_norm_kernel, columns),
        out_shape=(
            jax.ShapeDtypeStruct((tokens, width), BF16),
            jax.ShapeDtypeStruct((tokens, width), F32),
            jax.ShapeDtypeStruct((tokens, width), F32),
            jax.ShapeDtypeStruct((tokens, 1), F32),
            jax.ShapeDtypeStruct((2, width, half), BF16),
        ),
        in_specs=[pl.BlockSpec(memory_space=pltpu.SMEM)]
        + [vmem] * 3
        + [pl.BlockSpec(memory_space=pl.ANY)] * 2,
        out_specs=(vmem,) * 5,
        scratch_shapes=[pltpu.SemaphoreType.DMA((2,))],
        compiler_params=pltpu.CompilerParams(vmem_limit_bytes=VMEM_BYTES),
        cost_estimate=pl.CostEstimate(
            flops=64 * tokens * width * width, bytes_accessed=4 * width * width, transcendentals=0
        ),
        name="first_norm",
    )(core, mixed, rows, vectors, own, swap)


def ff_forward_kernel(
    in_columns,
    out_columns,
    core_ref,
    hidden_ref,
    bias_ref,
    own_ref,
    swap_ref,
    act_ref,
    slope_ref,
    gelu_ref,
    parts_ref,
    w_in_ref,
    w_out_ref,
    sems,
):
    in_copies = assemble(core_ref, own_ref, swap_ref, in_columns, w_in_ref, sems.at[0])
    out_copies = assemble(core_ref, own_ref, swap_ref, out_columns, w_out_ref, sems.at[1])
    for copy in in_copies:
        copy.wait()
    tokens = hidden_ref.shape[0]

    def expand(tile, carry):
        at = pl.ds(pl.multiple_of(tile * FF_TILE, FF_TILE), FF_TILE)
        rows = hidden_ref[at, :]
        gate = nn(rows, w_in_ref[0]) + bias_ref[0:1, :]
        up = nn(rows, w_in_ref[1]) + bias_ref[1:2, :]
        cdf = 0.5 * (1.0 + lax.erf(gate * (0.5**0.5)))
        density = jnp.exp(-0.5 * gate * gate) * 0.3989422804014327
        gelu = gate * cdf
        act_ref[at, :] = (gelu * up).astype(BF16)
        gelu_ref[at, :] = gelu.astype(BF16)
        slope_ref[at, :] = (up * (cdf + gate * density)).astype(BF16)
        return carry

    lax.fori_loop(0, tokens // FF_TILE, expand, 0)
    for copy in out_copies:
        copy.wait()

    def contract(tile, carry):
        at = pl.ds(pl.multiple_of(tile * FF_TILE, FF_TILE), FF_TILE)
        rows = act_ref[at, :]
        parts_ref[at, :] = jnp.concatenate(
            [nn(rows, w_out_ref[0]), nn(rows, w_out_ref[1])], axis=1
        ).astype(BF16)
        return carry

    lax.fori_loop(0, tokens // FF_TILE, contract, 0)


def ff_forward(core, hidden, bias, own, swap, in_columns, out_columns):
    tokens, width = hidden.shape
    units = bias.shape[1]
    vmem = pl.BlockSpec(memory_space=pltpu.VMEM)
    return pl.pallas_call(
        functools.partial(ff_forward_kernel, in_columns, out_columns),
        out_shape=(
            jax.ShapeDtypeStruct((tokens, units), BF16),
            jax.ShapeDtypeStruct((tokens, units), BF16),
            jax.ShapeDtypeStruct((tokens, units), BF16),
            jax.ShapeDtypeStruct((tokens, width), BF16),
            jax.ShapeDtypeStruct((2, width, units), BF16),
            jax.ShapeDtypeStruct((2, units, width // 2), BF16),
        ),
        in_specs=[pl.BlockSpec(memory_space=pltpu.SMEM)]
        + [vmem] * 2
        + [pl.BlockSpec(memory_space=pl.ANY)] * 2,
        out_specs=(vmem,) * 6,
        scratch_shapes=[pltpu.SemaphoreType.DMA((2, 2))],
        compiler_params=pltpu.CompilerParams(vmem_limit_bytes=VMEM_BYTES),
        cost_estimate=pl.CostEstimate(
            flops=32 * tokens * width * units,
            bytes_accessed=6 * width * units,
            transcendentals=2 * tokens * units,
        ),
        name="ff_forward",
    )(core, hidden, bias, own, swap)


def second_norm_kernel(
    parts_ref, hidden_ref, cotangent_ref, vec_ref, result_ref, grad_ref, low_ref, sums_ref
):
    lin = jnp.sum(parts_ref[...].astype(F32), axis=0) + vec_ref[5:6, :]
    normal, scale = normalised(hidden_ref[...] + lin)
    gain = vec_ref[6:7, :]
    result_ref[...] = (normal * gain + vec_ref[7:8, :]).astype(BF16)
    grads = cotangent_ref[...].astype(F32)
    back = norm_back(grads, normal, scale, gain)
    low = back.astype(BF16)
    grad_ref[...] = back
    low_ref[...] = low
    sums_ref[...] = jnp.concatenate(
        [
            column_sum(low.astype(F32)),
            column_sum(grads * normal),
            column_sum(grads),
            jnp.zeros((5, back.shape[1]), F32),
        ]
    )


def second_norm(parts, hidden, cotangent, vectors):
    tokens, width = hidden.shape
    vmem = pl.BlockSpec(memory_space=pltpu.VMEM)
    return pl.pallas_call(
        second_norm_kernel,
        out_shape=(
            jax.ShapeDtypeStruct((tokens, width), BF16),
            jax.ShapeDtypeStruct((tokens, width), F32),
            jax.ShapeDtypeStruct((tokens, width), BF16),
            jax.ShapeDtypeStruct((8, width), F32),
        ),
        in_specs=[vmem] * 4,
        out_specs=(vmem,) * 4,
        compiler_params=pltpu.CompilerParams(vmem_limit_bytes=VMEM_BYTES),
        cost_estimate=pl.CostEstimate(
            flops=20000 * tokens * width, bytes_accessed=20 * tokens * width, transcendentals=0
        ),
        name="second_norm",
    )(parts, hidden, cotangent, vectors)


def ff_backward_kernel(
    grad_ref, slope_ref, gelu_ref, w_in_ref, w_out_ref, joined_ref, parts_ref, bias_ref, half_ref
):
    tokens, width = grad_ref.shape
    half = width // 2
    bias_ref[...] = jnp.zeros_like(bias_ref)

    def visit(tile, carry):
        at = pl.ds(pl.multiple_of(tile * FF_TILE, FF_TILE), FF_TILE)
        left, right = grad_ref[at, :half], grad_ref[at, half:]
        half_ref[0, at, :] = left
        half_ref[1, at, :] = right
        act_grad = nt(left, w_out_ref[0]) + nt(right, w_out_ref[1])
        for which, factor in ((0, slope_ref), (1, gelu_ref)):
            joined = (act_grad * factor[at, :].astype(F32)).astype(BF16)
            joined_ref[which, at, :] = joined
            bias_ref[which : which + 1, :] += column_sum(joined.astype(F32))
        parts_ref[at, :] = (
            nt(joined_ref[0, at, :], w_in_ref[0]) + nt(joined_ref[1, at, :], w_in_ref[1])
        ).astype(BF16)
        return carry

    lax.fori_loop(0, tokens // FF_TILE, visit, 0)


def ff_backward(grads, slope, gelu, w_in, w_out):
    tokens, width = grads.shape
    units = slope.shape[1]
    vmem = pl.BlockSpec(memory_space=pltpu.VMEM)
    return pl.pallas_call(
        ff_backward_kernel,
        out_shape=(
            jax.ShapeDtypeStruct((2, tokens, units), BF16),
            jax.ShapeDtypeStruct((tokens, width), BF16),
            jax.ShapeDtypeStruct((2, units), F32),
            jax.ShapeDtypeStruct((2, tokens, width // 2), BF16),
        ),
        in_specs=[vmem] * 5,
        out_specs=(vmem,) * 4,
        compiler_params=pltpu.CompilerParams(vmem_limit_bytes=VMEM_BYTES),
        cost_estimate=pl.CostEstimate(
            flops=32 * tokens * width * units,
            bytes_accessed=6 * width * units,
            transcendentals=0,
        ),
        name="ff_backward",
    )(grads, slope, gelu, w_in, w_out)


def first_back_kernel(
    parts_ref,
    second_ref,
    normal_ref,
    scale_ref,
    vec_ref,
    weight_ref,
    sums_ref,
    _,
    __,
    grad_ref,
    low_ref,
    out_ref,
    turned_ref,
):
    tokens, width = second_ref.shape
    half, count = width // 2, tokens // 2
    normal = normal_ref[...]
    grads = second_ref[...] + jnp.sum(parts_ref[...].astype(F32), axis=0)
    back = norm_back(grads, normal, scale_ref[...], vec_ref[3:4, :])
    low = back.astype(BF16)
    grad_ref[...] = back
    low_ref[0] = low[:, :half]
    low_ref[1] = low[:, half:]
    out_grad = nt(low[:, :half], weight_ref[0]) + nt(low[:, half:], weight_ref[1])
    for seq in range(2):
        for group in range(GROUPS):
            out_ref[seq * GROUPS + group] = out_grad[
                seq * count : (seq + 1) * count, group * GROUP_WIDTH : (group + 1) * GROUP_WIDTH
            ].astype(BF16)
    rows = jnp.concatenate(
        [
            column_sum(low.astype(F32)),
            column_sum(grads * normal),
            column_sum(grads),
            sums_ref[0:3, :],
            jnp.zeros((122, width), F32),
        ]
    )
    turned_ref[...] = rows.T.astype(BF16)


def first_back(parts, second_grad, normal, scale, vectors, weight, sums, *earlier):
    tokens, width = second_grad.shape
    vmem = pl.BlockSpec(memory_space=pltpu.VMEM)
    return pl.pallas_call(
        first_back_kernel,
        out_shape=(
            jax.ShapeDtypeStruct((tokens, width), F32),
            jax.ShapeDtypeStruct((2, tokens, width // 2), BF16),
            jax.ShapeDtypeStruct((2 * GROUPS, tokens // 2, GROUP_WIDTH), BF16),
            jax.ShapeDtypeStruct((width, 128), BF16),
        ),
        in_specs=[vmem] * 7 + [pl.BlockSpec(memory_space=pl.ANY)] * 2,
        out_specs=(vmem,) * 4,
        compiler_params=pltpu.CompilerParams(vmem_limit_bytes=VMEM_BYTES),
        cost_estimate=pl.CostEstimate(
            flops=64 * tokens * width * width, bytes_accessed=4 * width * width, transcendentals=0
        ),
        name="first_back",
    )(parts, second_grad, normal, scale, vectors, weight, sums, *earlier)


def swap_sum(keep, give, axis):
    return keep.astype(F32) + lax.ppermute(give.astype(BF16), axis, SWAP).astype(F32)


def gather_plane(block):
    return lax.all_gather(block, PLANE, axis=0, tiled=True)


def spread_plane(parts):
    return lax.all_to_all(parts.reshape(4, -1, parts.shape[1]), PLANE, 0, 0, tiled=True)


def after(array, earlier):
    first = earlier[(slice(0, 1),) * earlier.ndim].reshape((1,) * array.ndim)
    return array + (first.astype(F32) * 0.0).astype(array.dtype)


def hold_kernel(*refs):
    del refs


def hold(array, earlier):
    anywhere = pl.BlockSpec(memory_space=pl.ANY)
    return pl.pallas_call(
        hold_kernel,
        out_shape=jax.ShapeDtypeStruct(array.shape, array.dtype),
        in_specs=[anywhere] * 2,
        out_specs=anywhere,
        input_output_aliases={0: 0},
        name="hold",
    )(array, earlier)


def pick(parts, index):
    return lax.dynamic_index_in_dim(parts, index, 0, keepdims=False)


def two(own, other, index):
    return jnp.where(index == 0, jnp.stack([own, other]), jnp.stack([other, own]))


def body(
    tokens,
    positions,
    w_qkv,
    qv_bias,
    w_attn_out,
    attn_out_bias,
    norm1_gain,
    norm1_bias,
    w_in,
    in_bias,
    w_out,
    out_bias,
    norm2_gain,
    norm2_bias,
    cotangent,
):
    seq_count, row_count, width = tokens.shape
    outer = lax.axis_size("e")
    seq_size = 2 * outer * GROUPS
    devices = seq_size * 4
    shard = w_qkv.shape[0]
    ff_shard = w_out.shape[0]
    ring = 4 * outer
    group = lax.axis_index(("r", "x"))
    place = lax.axis_index(("y", "c"))
    units = 2 * ring * ff_shard
    y_at, c_at = lax.axis_index("y"), lax.axis_index("c")
    qkv_cols = 3 * GROUP_WIDTH

    with jax.named_scope("gather_qkv_weights"):
        own_pos = lax.dynamic_slice_in_dim(positions, place * row_count, row_count, 1)
        shorts = jnp.stack(
            [
                qv_bias[0],
                qv_bias[1],
                attn_out_bias,
                norm1_gain,
                norm1_bias,
                out_bias,
                norm2_gain,
                norm2_bias,
            ]
        )
        wide = -(-qkv_cols // 128) * 128
        longs = jnp.concatenate(
            [
                jnp.pad(own_pos >> 7, ((0, 0), (0, wide - 128 - row_count))).astype(BF16)[:, None],
                jnp.pad(own_pos & 127, ((0, 0), (0, wide - 128 - row_count))).astype(BF16)[:, None],
                jnp.broadcast_to(
                    jnp.pad(in_bias, (0, wide - 128 - 2 * ff_shard)), (2, 1, wide - 128)
                ),
                jnp.zeros((2, 5, wide - 128), BF16),
            ],
            axis=1,
        )
        smalls = jnp.concatenate(
            [jnp.broadcast_to(jnp.pad(shorts, ((0, 0), (0, 128 - shard))), (2, 8, 128)), longs],
            axis=2,
        )
        columns = (
            w_qkv.reshape(shard, 3, GROUPS, GROUP_WIDTH)
            .transpose(2, 0, 1, 3)
            .reshape(1, GROUPS, shard, qkv_cols)
        )
        columns = jnp.pad(columns, ((0, 0), (0, 0), (0, 0), (0, wide - qkv_cols)))
        parcel = jnp.concatenate(
            [
                jnp.broadcast_to(columns, (2, GROUPS, shard, wide)),
                jnp.broadcast_to(smalls[:, None], (2, GROUPS, 8, wide)),
            ],
            axis=2,
        ).reshape(8, shard + 8, wide)
        parcel = lax.all_to_all(parcel, SEQ_GROUP, 0, 0, tiled=True)

    with jax.named_scope("gather_tokens"):
        s_at, r_at, x_at = (lax.axis_index(name) for name in SEQ_GROUP)
        chunk = two(
            pick(tokens, s_at), lax.ppermute(pick(tokens, 1 - s_at), "s", SWAP), s_at
        )
        chunk = after(chunk, parcel)
        chunk = two(chunk, lax.ppermute(chunk, "r", SWAP), r_at)
        chunk = two(chunk, lax.ppermute(chunk, "x", SWAP), x_at)
        chunk = chunk.transpose(2, 1, 0, 3, 4).reshape(8 * row_count, width)

    with jax.named_scope("gather_qkv_weights"):
        sent = parcel
        parcel = two(parcel, lax.ppermute(parcel, "y", SWAP), y_at)
        parcel = two(parcel, lax.ppermute(parcel, "c", SWAP), c_at)
        parcels = parcel[None]
        if outer > 1:
            parcels = lax.all_gather(parcel, "e", axis=0, tiled=False)
        parcels = parcels.reshape(outer, 2, 2, 2, 2, 2, shard + 8, wide)
        order = (3, 0, 4, 5, 2, 1)
        qkv_slice = (
            parcels[..., :shard, :qkv_cols].transpose(*order, 6, 7).reshape(width, qkv_cols)
        )
        vectors = (
            parcels[..., shard:, :shard].transpose(6, *order, 7).reshape(8, width).astype(F32)
        )
        pos_parts = parcels[..., shard : shard + 2, 128 : 128 + row_count].astype(F32)
        chunk_pos = (pos_parts[..., 0, :] * 128.0 + pos_parts[..., 1, :]).reshape(
            outer, 2, 2, 8 * row_count
        )
        in_shift = lax.dynamic_index_in_dim(
            lax.dynamic_index_in_dim(
                parcels[..., shard + 2, 128 : 128 + 2 * ff_shard], y_at, 1, keepdims=False
            ),
            x_at,
            1,
            keepdims=False,
        )
        in_shift = (
            in_shift.transpose(1, 0, 2, 3, 4).reshape(2, units).astype(F32)
        )

    with jax.named_scope("gather_ff_weights"):
        half = width // 2
        in_cols = (
            w_in.reshape(shard, 2, ring, 4, 2 * ff_shard)
            .transpose(3, 1, 0, 2, 4)
            .reshape(4, 2, shard, units)
        )
        attn_cols = w_attn_out.reshape(shard, 2, half).transpose(1, 0, 2)
        in_parts = jnp.concatenate(
            [in_cols, jnp.broadcast_to(attn_cols, (4, 2, shard, half))], axis=3
        ).reshape(8, shard, units + half)
        in_parts = lax.all_to_all(after(in_parts, sent), ("x", "y", "c"), 0, 0, tiled=True)
        out_halves = w_out.reshape(ff_shard, 2, half).transpose(1, 0, 2)
        out_cols = two(
            pick(out_halves, c_at), lax.ppermute(pick(out_halves, 1 - c_at), "c", SWAP), c_at
        ).reshape(2 * ff_shard, half)
        packed = jnp.concatenate(
            [in_parts.reshape(8 * shard, units + half), out_cols], axis=1
        )
        packed = lax.all_gather(packed, RING, axis=0, tiled=True)
        core = c_at.reshape(1).astype(jnp.int32)

    with jax.named_scope("project"):
        qv_slice = lax.dynamic_slice_in_dim(vectors[:2], group * GROUP_WIDTH, GROUP_WIDTH, 1)
        column_bias = jnp.concatenate(
            [qv_slice[0], jnp.zeros((GROUP_WIDTH,), F32), qv_slice[1]]
        )
        turned_chunk = (
            chunk.reshape(8 * row_count, seq_size, 2, 2, shard)
            .transpose(0, 3, 2, 1, 4)
            .reshape(8 * row_count, width)
        )
        queries = (
            jnp.dot(chunk, qkv_slice[:, :GROUP_WIDTH], preferred_element_type=F32)
            + column_bias[:GROUP_WIDTH]
        ).astype(BF16)
        own_kv = (
            jnp.dot(chunk, qkv_slice[:, GROUP_WIDTH:], preferred_element_type=F32)
            + column_bias[GROUP_WIDTH:]
        ).astype(BF16)
    with jax.named_scope("gather_kv"):
        if outer > 1:
            own_kv = lax.all_gather(own_kv, "e", axis=0, tiled=True)
        y_kv = lax.ppermute(own_kv, "y", SWAP)
        key_values = [
            own_kv,
            lax.ppermute(own_kv, "c", SWAP),
            y_kv,
            lax.ppermute(y_kv, "c", SWAP),
        ]
    ordered_pos = jnp.stack(
        [
            lax.dynamic_index_in_dim(
                lax.dynamic_index_in_dim(chunk_pos, c_at ^ kc, 1, keepdims=False),
                y_at ^ ky,
                1,
                keepdims=False,
            )
            for ky in (0, 1)
            for kc in (0, 1)
        ]
    )
    query_pos = lax.dynamic_index_in_dim(ordered_pos[0], lax.axis_index("e"), 0, keepdims=True)
    key_pos = ordered_pos.reshape(4 * outer, 8 * row_count)
    head_ids = group * GROUP_HEADS + jnp.arange(GROUP_HEADS)
    slopes = 2.0 ** (-8.0 * (head_ids + 1).astype(F32) / HEADS) * LOG2E

    with jax.named_scope("attention"):
        near = 2 * outer
        state = attend(
            slopes, queries, query_pos, key_pos[:near], key_values[:2], None, last=False
        )
        attended, log_sums, attended_low = attend(
            slopes, queries, query_pos, key_pos[near:], key_values[2:], state, last=True
        )

    with jax.named_scope("return_attended"):
        returned = lax.all_to_all(
            attended_low.reshape(8, row_count, GROUP_WIDTH), SEQ_GROUP, 0, 0, tiled=True
        )
        mixed = (
            returned.reshape(2, GROUPS, row_count, GROUP_WIDTH)
            .transpose(0, 2, 1, 3)
            .reshape(2 * row_count, width)
        )
    with jax.named_scope("first_norm"):
        packed = hold(packed, mixed)
        attn_own = packed[:, units : units + half]
        attn_swap = lax.ppermute(attn_own, "c", SWAP)
        hidden_low, hidden, normal, scale, attn_full = first_norm(
            core,
            mixed,
            tokens.reshape(2 * row_count, width),
            vectors,
            attn_own,
            attn_swap,
            slice(None),
        )
        swapped = lax.ppermute(hold(packed, hidden_low), "c", SWAP)
    with jax.named_scope("gather_hidden"):
        hidden_group = gather_plane(hidden_low)
    with jax.named_scope("ff_forward"):
        activated_low, slope, gelu, ff_parts, in_slice, out_slice = ff_forward(
            core,
            hidden_group,
            in_shift,
            packed,
            swapped,
            slice(0, units),
            slice(units + half, units + width),
        )
    with jax.named_scope("sum_ff"):
        ff_parts = spread_plane(ff_parts)
    with jax.named_scope("second_norm"):
        result, second_grad, ff_grad, sums = second_norm(
            ff_parts, hidden, cotangent.reshape(2 * row_count, width), vectors
        )
    with jax.named_scope("gather_ff_grad"):
        ff_grads = gather_plane(ff_grad)
    with jax.named_scope("ff_backward"):
        joined_grad, hidden_parts, grad_in_shift, grad_halves = ff_backward(
            ff_grads, slope, gelu, in_slice, out_slice
        )
    with jax.named_scope("sum_hidden_grad"):
        hidden_parts = spread_plane(hidden_parts)
    with jax.named_scope("ff_weight_grads"):
        in_rows = swap_sum(
            tn(hidden_group, pick(joined_grad, c_at)),
            tn(hidden_group, pick(joined_grad, 1 - c_at)),
            "c",
        ).astype(BF16)
        out_rows = swap_sum(
            tn(activated_low, pick(grad_halves, c_at)),
            tn(activated_low, pick(grad_halves, 1 - c_at)),
            "c",
        ).astype(BF16)
        grad_in_rows = lax.psum_scatter(in_rows, RING, scatter_dimension=0, tiled=True)
        grad_out_rows = lax.psum_scatter(
            hold(out_rows, in_rows), RING, scatter_dimension=0, tiled=True
        ).reshape(2, ff_shard, half)
        grad_w_out = (
            two(
                pick(grad_out_rows, c_at),
                lax.ppermute(pick(grad_out_rows, 1 - c_at), "c", SWAP),
                c_at,
            )
            .transpose(1, 0, 2)
            .reshape(ff_shard, width)
            .astype(F32)
        )
        grad_in_rows = lax.all_to_all(
            grad_in_rows.reshape(8, shard, -1), ("x", "y", "c"), 0, 0, tiled=True
        )
        grad_w_in = (
            grad_in_rows.reshape(4, 2, shard, ring, 2 * ff_shard)
            .transpose(2, 1, 3, 0, 4)
            .reshape(shard, 2 * devices * ff_shard)
            .astype(F32)
        )
    with jax.named_scope("first_norm_back"):
        first_grad, attn_grad, out_grad, turned = first_back(
            hidden_parts,
            second_grad,
            normal,
            scale,
            vectors,
            attn_full,
            sums,
            in_rows,
            out_rows,
        )
    with jax.named_scope("send_out_grad"):
        out_grads = lax.all_to_all(
            out_grad,
            SEQ_GROUP,
            0,
            0,
            tiled=True,
        ).reshape(8 * row_count, GROUP_WIDTH)
    with jax.named_scope("attn_weight_grad"):
        give = jnp.concatenate(
            [tn(mixed, pick(attn_grad, 1 - c_at)).astype(BF16), turned], axis=1
        )
        keep = jnp.concatenate([tn(mixed, pick(attn_grad, c_at)), turned.astype(F32)], axis=1)
        attn_rows = swap_sum(keep, give, "c").astype(BF16)
        rows_out = lax.psum_scatter(attn_rows, RING, scatter_dimension=0, tiled=True)
        rows_out = rows_out.reshape(4, 2, shard, -1).transpose(1, 0, 2, 3)
        rows_out = two(
            pick(rows_out, c_at), lax.ppermute(pick(rows_out, 1 - c_at), "c", SWAP), c_at
        ).reshape(2, 2, 2, shard, -1)
        rows_out = swap_sum(
            lax.dynamic_index_in_dim(rows_out, y_at, 2, keepdims=False),
            lax.dynamic_index_in_dim(rows_out, 1 - y_at, 2, keepdims=False),
            "y",
        )
        rows_out = swap_sum(
            lax.dynamic_index_in_dim(rows_out, x_at, 1, keepdims=False),
            lax.dynamic_index_in_dim(rows_out, 1 - x_at, 1, keepdims=False),
            "x",
        )
        grad_w_attn = rows_out[..., :half].transpose(1, 0, 2).reshape(shard, width)
        vector_grads = rows_out[0, :, half : half + 8].T

    with jax.named_scope("attention_back"):
        state, y_part, cy_part = attend_back(
            slopes,
            queries,
            query_pos,
            key_pos[near:],
            out_grads,
            attended,
            log_sums,
            key_values[2:],
            None,
            last=False,
            earlier=attn_rows,
        )
        y_sum = swap_sum(y_part, cy_part, "c").astype(BF16)
        query_grads, own_part, c_part = attend_back(
            slopes,
            queries,
            query_pos,
            key_pos[:near],
            out_grads,
            attended,
            log_sums,
            key_values[:2],
            state,
            last=True,
            earlier=y_sum,
        )
    with jax.named_scope("sum_kv_grads"):
        kv_grads = swap_sum(swap_sum(own_part, c_part, "c"), y_sum, "y")
        if outer > 1:
            kv_grads = lax.psum_scatter(kv_grads, "e", scatter_dimension=0, tiled=True)
        qkv_grad = jnp.concatenate([query_grads, kv_grads.astype(BF16)], axis=1)

    with jax.named_scope("input_grad"):
        input_parts = nt(qkv_grad, qkv_slice).astype(BF16).reshape(8, row_count, width)
        input_parts = lax.all_to_all(input_parts, SEQ_GROUP, 0, 0, tiled=True)
        input_grad = first_grad.reshape(2, row_count, width) + jnp.sum(
            input_parts.reshape(2, GROUPS, row_count, width).astype(F32), axis=1
        )
    with jax.named_scope("qkv_weight_grad"):
        blocks = tn(turned_chunk, qkv_grad).reshape(2, 2, seq_size, shard, qkv_cols)
        column_sums = jnp.sum(qkv_grad.astype(F32), axis=0)
        rows_at = jnp.arange(8)[None, None, None, :, None]
        here = (jnp.arange(2)[:, None] == y_at) & (jnp.arange(2)[None, :] == x_at)
        shifts = jnp.pad(grad_in_shift.reshape(seq_size, 2 * ff_shard), ((0, 0), (0, qkv_cols - 2 * ff_shard)))
        smalls = jnp.where(
            rows_at == 0,
            column_sums[None, None, None, None, :],
            jnp.where(
                (rows_at == 1) & here[:, :, None, None, None], shifts[None, None, :, None, :], 0.0
            ),
        )
        bundle = jnp.concatenate([blocks, smalls], axis=3)
        bundle = swap_sum(pick(bundle, c_at), pick(bundle, 1 - c_at), "c")
        bundle = swap_sum(pick(bundle, y_at), pick(bundle, 1 - y_at), "y")
        shares = lax.all_to_all(bundle.astype(BF16), SEQ_AXIS, 0, 0, tiled=True).astype(F32)
        totals = jnp.sum(shares.reshape(2 * outer, GROUPS, shard + 8, qkv_cols), axis=0)
        grad_w_qkv = (
            totals[:, :shard]
            .reshape(GROUPS, shard, 3, GROUP_WIDTH)
            .transpose(1, 2, 0, 3)
            .reshape(shard, 3 * width)
        )
        sums = totals[:, shard].reshape(GROUPS, 3, GROUP_WIDTH).transpose(1, 0, 2).reshape(3, width)
        grad_qv = lax.dynamic_slice_in_dim(sums[0::2], lax.axis_index(EVERY) * shard, shard, 1)
        grad_in_bias = jnp.sum(totals[:, shard + 1, : 2 * ff_shard], axis=0)

    return (
        result.reshape(2, row_count, width).astype(BF16),
        input_grad,
        grad_w_qkv,
        grad_qv,
        grad_w_attn,
        vector_grads[0],
        vector_grads[1],
        vector_grads[2],
        grad_w_in,
        grad_in_bias,
        grad_w_out,
        vector_grads[3],
        vector_grads[4],
        vector_grads[5],
    )


def solution(mesh):
    seq_size = mesh.shape["seq"]
    split = Mesh(mesh.devices.reshape(2, seq_size // 8, 2, 2, 2, 2), EVERY)
    tokens_at = P(None, EVERY, None)
    rows_at = P(EVERY, None)
    vector_at = P(EVERY)
    return jax.shard_map(
        body,
        mesh=split,
        in_specs=(
            tokens_at,
            P(None, SEQ_AXIS),
            rows_at,
            P(None, EVERY),
            rows_at,
            vector_at,
            vector_at,
            vector_at,
            rows_at,
            vector_at,
            rows_at,
            vector_at,
            vector_at,
            vector_at,
            tokens_at,
        ),
        out_specs=(
            tokens_at,
            tokens_at,
            rows_at,
            P(None, EVERY),
            rows_at,
            vector_at,
            vector_at,
            vector_at,
            rows_at,
            vector_at,
            rows_at,
            vector_at,
            vector_at,
            vector_at,
        ),
        check_vma=False,
    )
```

time: 457 us -> 324 us (0.71)
  waiting for transfers between devices: 269 us -> 76.2 us
  blocking collectives: 23.8 us -> 61 us
  Pallas kernels: 25.6 us -> 50.5 us
  starting transfers between devices: 38.1 us -> 46.6 us
  local copies, waits for them, and re-layouts: 37.3 us -> 29 us
    reduce_scatter x4 -> x3, waiting for transfers between devices: 143 us -> 13.6 us  [the longest x1 13.6 us: body(): lax.psum_scatter(attn_rows, RING, scatter_dimension=0, tiled=True)]
    all_gather x3 -> x1, waiting for transfers between devices: 41.4 us -> 3.68 us  [body(): packed = lax.all_gather(packed, RING, axis=0, tiled=True)]
    pallas_call x2 -> x12, Pallas kernels: 25.6 us -> 50.5 us  [the longest x2 14.3 us: attend_back(): pl.pallas_call(functools.partial(attend_back_kernel, count, first, last),...]
    all_to_all x1 -> x2, blocking collectives: 15 us -> 35.2 us  [the longest x1 20.2 us: body(): lax.all_to_all(attended_low.reshape(8, row_count, GROUP_WIDTH), SEQ_GROUP...]
    all_gather x1 -> x2, blocking collectives: 8.87 us -> 25.8 us  [gather_plane(): return lax.all_gather(block, PLANE, axis=0, tiled=True)]
    ppermute x13 -> x23, waiting for transfers between devices: 38 us -> 27.3 us  [the longest x1 9.96 us: body(): parcel = two(parcel, lax.ppermute(parcel, 'y', SWAP), y_at)]
    ppermute x13 -> x23, starting transfers between devices: 7.82 us -> 16.1 us  [the longest x10 6.76 us: swap_sum(): lax.ppermute(give.astype(BF16), axis, SWAP).astype(F32)]
    reduce_sum x13 -> x2, other arithmetic: 7.42 us -> 0.63 us  [the longest x1 0.59 us: body(): grad_in_bias = jnp.sum(totals[:, shard + 1, :2 * ff_shard], axis=0)]
  transfers between devices with their start and end apart: 27 -> 34, of which waited for: 22 -> 14; matrix products, arithmetic and copies ran while one was open for 13% -> 17% of each run, Pallas kernels for 6% -> 9%
where the time goes in v2:
time: 324 us; the launch traced here: 319 us
  waiting for transfers between devices  76.2 us (24%)
  blocking collectives  61 us (19%)
  Pallas kernels  50.5 us (16%)
  starting transfers between devices  46.6 us (14%)
  local copies, waits for them, and re-layouts  29 us (9%)
  other arithmetic  20.6 us (6%)
  matrix products  19.2 us (6%)
  between operations  15.6 us (5%)
    all_gather x2, blocking collectives, gather_plane(): return lax.all_gather(block, PLANE, axis=0, tiled=True)  25.8 us
    all_to_all x1, blocking collectives, body(): lax.all_to_all(attended_low.reshape(8, row_count, GROUP_WIDTH), SEQ_GROUP...  20.2 us
    all_to_all x1, blocking collectives, spread_plane(): lax.all_to_all(parts.reshape(4, -1, parts.shape[1]), PLANE, 0, 0, tiled=T...  15 us
    pallas_call x2, Pallas kernels, attend_back(): pl.pallas_call(functools.partial(attend_back_kernel, count, first, last),...  14.3 us
    reduce_scatter x1, waiting for transfers between devices, body(): lax.psum_scatter(attn_rows, RING, scatter_dimension=0, tiled=True)  13.6 us
    dot_general x7, matrix products, tn(): lax.dot_general(a, b, (((0,), (0,)), ((), ())), preferred_element_type=F32)  11.5 us
    pallas_call x2, Pallas kernels, attend(): pl.pallas_call(functools.partial(attend_kernel, count, first, last), out_...  11.4 us
    ppermute x1, waiting for transfers between devices, body(): parcel = two(parcel, lax.ppermute(parcel, 'y', SWAP), y_at)  9.96 us
  transfers between devices with their start and end apart: 34, of which 14 were waited for; matrix products, arithmetic and copies ran while one was open for 17% of the time, Pallas kernels for 9%

profile of v2, /device:TPU:0, one launch (start us, length us, event | category | flops | bytes accessed | tf_op | source)
XLA Modules:
  0.0 318.8 jit_solution(13155608961777502557)
XLA Ops:
  9.5 1.1 reshape.630
  11.7 7.4 %all-to-all-start = ((bf16[8,32,640]{2,1,0:T(8,128)(2,1)}), bf16[8,32,640]{2,1,0:T(8,128)(2,1)S(1)}, u32[]{:S(2)}, u32[]{:S(2)}) async-start(bf16[8,32,640]{2,1,0:T(8,128)(2,1)} %bitcast.15), calls=%async_computation | async-start | bytes 655360 | tf_op jit(solution)/shard_map/gather_qkv_weights/all_to_all | solution.py:695
  19.6 3.0 collective-permute-start
  24.2 8.4 %all-to-all-done = bf16[8,32,640]{2,1,0:T(8,128)(2,1)S(1)} async-done(((bf16[8,32,640]{2,1,0:T(8,128)(2,1)}), bf16[8,32,640]{2,1,0:T(8,128)(2,1)S(1)}, u32[]{:S(2)}, u32[]{:S(2)}) %all-to-all-start) | async-done | bytes 327712 | tf_op jit(solution)/shard_map/gather_qkv_weights/all_to_all | solution.py:695
  35.2 3.5 %all-to-all-start.2 = ((bf16[8,24,1152]{2,1,0:T(8,128)(2,1)}), bf16[8,24,1152]{2,1,0:T(8,128)(2,1)S(1)}, u32[]{:S(2)}, u32[]{:S(2)}) async-start(bf16[8,24,1152]{2,1,0:T(8,128)(2,1)} %maximum_add_fusion.1), calls=%async_computation.2 | async-start | bytes 884736 | tf_op jit(solution)/shard_map/gather_ff_weights/all_to_all | solution.py:749
  39.3 1.9 collective-permute-start.3
  42.1 1.5 collective-permute-start.2
  43.6 10.0 %collective-permute-done.3 = bf16[8,32,640]{2,1,0:T(8,128)(2,1)S(1)} collective-permute-done((bf16[8,32,640]{2,1,0:T(8,128)(2,1)S(1)}, bf16[8,32,640]{2,1,0:T(8,128)(2,1)S(1)}, u32[]{:S(2)}, u32[]{:S(2)}) %collective-permute-start.3) | collective-permute-done | bytes 327712 | tf_op jit(solution)/shard_map/gather_qkv_weights/ppermute | solution.py:709
  55.0 1.0 maximum_select_fusion.1
  56.0 1.5 maximum_select_fusion
  58.1 2.6 fusion.7.refs_0_
  61.0 1.1 collective-permute-start.5
  64.1 2.2 fusion.8.q_ref
  66.3 6.2 %collective-permute-done.5.refs_0_ = bf16[512,384]{1,0:T(8,128)(2,1)} collective-permute-done((bf16[512,384]{1,0:T(8,128)(2,1)}, bf16[512,384]{1,0:T(8,128)(2,1)}, u32[]{:S(2)}, u32[]{:S(2)}) %collective-permute-start.5) | collective-permute-done | bytes 393248 | tf_op jit(solution)/shard_map/gather_kv/ppermute | solution.py:781
  72.5 5.4 %attend.2 = (f32[192,512]{1,0:T(8,128)}, f32[6,512]{1,0:T(8,128)}) custom-call(f32[3]{0:T(128)} %power_multiply_fusion.slopes_ref, bf16[512,192]{1,0:T(8,128)(2,1)} %fusion.8.q_ref, f32[1,512]{1,0:T(1,128)} %get-tuple-element.102.pq_ref, f32[2,512]{1,0:T(2,128)} %maximum_bitcast_fusion.1.pk_ref, bf16[512,384]{1,0:T(8,128)(2,1)} %fusion.7.refs_0_, ...), custom_call_target="tpu_custom_call" | custom-call | flops 6442450944 | bytes 524288 | tf_op jit(solution)/shard_map/attention/attend/pallas_call | solution.py:143
  78.6 6.0 %attend.3 = (f32[192,512]{1,0:T(8,128)}, f32[3,512]{1,0:T(4,128)}, bf16[512,192]{1,0:T(8,128)(2,1)}) custom-call(f32[3]{0:T(128)} %power_multiply_fusion.slopes_ref, bf16[512,192]{1,0:T(8,128)(2,1)} %fusion.8.q_ref, f32[1,512]{1,0:T(1,128)} %get-tuple-element.102.pq_ref, f32[2,512]{1,0:T(2,128)} %maximum_bitcast_fusion.pk_ref, ...), custom_call_target="tpu_custom_call" | custom-call | flops 6442450944 | bytes 524288 | tf_op jit(solution)/shard_map/attention/attend/pallas_call | solution.py:143
  84.6 20.2 %all_to_all.45 = bf16[8,64,192]{2,1,0:T(8,128)(2,1)S(1)} all-to-all(bf16[8,64,192]{2,1,0:T(8,128)(2,1)} %bitcast.226), channel_id=1, replica_groups=mesh['s'=2,'e'=1,'r'=2,'x'=2,'y'=2,'c'=2] {'s','r','x'}, dimensions={0} | all-to-all | bytes 393216 | tf_op jit(solution)/shard_map/return_attended/all_to_all | solution.py:815
  105.9 3.7 %all-gather.2.cloned.1.call-done.refs_0_ = bf16[768,1536]{1,0:T(8,128)(2,1)} async-done(((bf16[192,1536]{1,0:T(8,128)(2,1)}), bf16[768,1536]{1,0:T(8,128)(2,1)}) %all-gather.2.cloned.1.call-update) | async-done | bytes 2359312 | tf_op jit(solution)/shard_map/gather_ff_weights/all_gather | solution.py:757
  109.6 1.1 slice.131.own_ref
  111.8 3.3 %copy.134.refs_0_ = bf16[768,1536]{1,0:T(8,128)(2,1)} copy(bf16[768,1536]{1,0:T(8,128)(2,1)} %hold.3.own_ref) | data formatting | bytes 4718592
  115.0 4.2 %first_norm.1 = (bf16[128,768]{1,0:T(8,128)(2,1)}, f32[128,768]{1,0:T(8,128)}, f32[128,768]{1,0:T(8,128)}, f32[128,1]{1,0:T(8,128)}, bf16[2,768,384]{2,1,0:T(8,128)(2,1)}) custom-call(s32[1]{0:T(128)} %bitcast.core_ref, bf16[128,768]{1,0:T(8,128)(2,1)} %reshape.637.refs_1_.mixed_ref, bf16[128,768]{1,0:T(8,128)(2,1)} %bitcast.227, ...), custom_call_target="tpu_custom_call" | custom-call | flops 4831838208 | bytes 2359296 | tf_op jit(solution)/shard_map/first_norm/first_norm/pallas_call | solution.py:325
  120.6 13.3 %all_gather.10.hidden_ref = bf16[512,768]{1,0:T(8,128)(2,1)} all-gather(bf16[128,768]{1,0:T(8,128)(2,1)S(1)} %copy-done.6), channel_id=1, replica_groups=mesh['s'=2,'e'=1,'r'=2,'x'=2,'y'=2,'c'=2] {'x','y'}, dimensions={0}, use_global_device_ids=true | all-gather | bytes 983040 | tf_op jit(solution)/shard_map/gather_hidden/all_gather | solution.py:586
  133.9 7.9 %ff_forward.1 = (bf16[512,768]{1,0:T(8,128)(2,1)}, bf16[512,768]{1,0:T(8,128)(2,1)}, bf16[512,768]{1,0:T(8,128)(2,1)}, bf16[512,768]{1,0:T(8,128)(2,1)}, bf16[2,...) custom-call(s32[1]{0:T(128)} %bitcast.core_ref, bf16[512,768]{1,0:T(8,128)(2,1)} %all_gather.10.hidden_ref, ...), custom_call_target="tpu_custom_call" | custom-call | flops 9663676416 | bytes 3538944 | tf_op jit(solution)/shard_map/ff_forward/ff_forward/pallas_call | solution.py:401
  141.8 15.0 %all_to_all.46.parts_ref = bf16[4,128,768]{2,1,0:T(8,128)(2,1)} all-to-all(bf16[4,128,768]{2,1,0:T(8,128)(2,1)} %bitcast.215), channel_id=1, replica_groups=mesh['s'=2,'e'=1,'r'=2,'x'=2,'y'=2,'c'=2] {'x','y'}, dimensions={0} | all-to-all | bytes 1572864 | tf_op jit(solution)/shard_map/sum_ff/all_to_all | solution.py:590
  156.8 2.5 second_norm.1
  159.3 12.5 %all_gather.11.grad_ref = bf16[512,768]{1,0:T(8,128)(2,1)} all-gather(bf16[128,768]{1,0:T(8,128)(2,1)} %get-tuple-element.55), channel_id=1, replica_groups=mesh['s'=2,'e'=1,'r'=2,'x'=2,'y'=2,'c'=2] {'x','y'}, dimensions={0}, use_global_device_ids=true | all-gather | bytes 983040 | tf_op jit(solution)/shard_map/gather_ff_grad/all_gather | solution.py:586
  171.8 6.9 %ff_backward.1 = (bf16[2,512,768]{2,1,0:T(8,128)(2,1)}, bf16[512,768]{1,0:T(8,128)(2,1)}, f32[2,768]{1,0:T(2,128)}, bf16[2,512,384]{2,1,0:T(8,128)(2,1)}) custom-call(bf16[512,768]{1,0:T(8,128)(2,1)} %all_gather.11.grad_ref, bf16[512,768]{1,0:T(8,128)(2,1)} %get-tuple-element.56.slope_ref, bf16[512,768]{1,0:T(8,128)(2,1)} %get-tuple-element.57.gelu_ref, ...), custom_call_target="tpu_custom_call" | custom-call | flops 9663676416 | bytes 3538944 | tf_op jit(solution)/shard_map/ff_backward/ff_backward/pallas_call | solution.py:498
  178.7 3.1 convolution_convert_fusion
  183.0 3.5 %all-to-all-start.4 = ((bf16[4,128,768]{2,1,0:T(8,128)(2,1)}), bf16[4,128,768]{2,1,0:T(8,128)(2,1)S(1)}, u32[]{:S(2)}, u32[]{:S(2)}) async-start(bf16[4,128,768]{2,1,0:T(8,128)(2,1)} %bitcast.56), calls=%async_computation.4 | async-start | bytes 1572864 | tf_op jit(solution)/shard_map/sum_hidden_grad/all_to_all | solution.py:590
  186.5 2.1 fusion.1.__
  189.6 3.1 add_convert_fusion._.refs_1_
  192.8 5.0 %all-to-all-done.4.parts_ref = bf16[4,128,768]{2,1,0:T(8,128)(2,1)S(1)} async-done(((bf16[4,128,768]{2,1,0:T(8,128)(2,1)}), bf16[4,128,768]{2,1,0:T(8,128)(2,1)S(1)}, u32[]{:S(2)}, u32[]{:S(2)}) %all-to-all-start.4) | async-done | bytes 786464 | tf_op jit(solution)/shard_map/sum_hidden_grad/all_to_all | solution.py:590
  197.7 0.9 copy-done.7
  198.7 3.4 %first_back.1 = (f32[128,768]{1,0:T(8,128)}, bf16[2,128,384]{2,1,0:T(8,128)(2,1)}, bf16[8,64,192]{2,1,0:T(8,128)(2,1)}, bf16[768,128]{1,0:T(8,128)(2,1)}) custom-call(bf16[4,128,768]{2,1,0:T(8,128)(2,1)} %copy-done.7, f32[128,768]{1,0:T(8,128)} %get-tuple-element.61.second_ref, f32[128,768]{1,0:T(8,128)} %get-tuple-element.62.normal_ref, ...), custom_call_target="tpu_custom_call" | custom-call | flops 4831838208 | bytes 2359296 | tf_op jit(solution)/shard_map/first_norm_back/first_back/pallas_call | solution.py:563
  202.1 1.3 convolution_convert_fusion.2
  203.4 1.0 pad_maximum_fusion
  204.5 4.1 %all-to-all-start.5 = ((bf16[8,64,192]{2,1,0:T(8,128)(2,1)}), bf16[8,64,192]{2,1,0:T(8,128)(2,1)}, u32[]{:S(2)}, u32[]{:S(2)}) async-start(bf16[8,64,192]{2,1,0:T(8,128)(2,1)} %get-tuple-element.70), calls=%async_computation.5 | async-start | bytes 524288 | tf_op jit(solution)/shard_map/send_out_grad/all_to_all | solution.py:910
  209.6 2.2 fusion._
  211.8 6.8 %all-to-all-done.5 = bf16[8,64,192]{2,1,0:T(8,128)(2,1)} async-done(((bf16[8,64,192]{2,1,0:T(8,128)(2,1)}), bf16[8,64,192]{2,1,0:T(8,128)(2,1)}, u32[]{:S(2)}, u32[]{:S(2)}) %all-to-all-start.5) | async-done | bytes 196640 | tf_op jit(solution)/shard_map/send_out_grad/all_to_all | solution.py:910
  218.6 7.0 %attend_back.2 = (f32[192,512]{1,0:T(8,128)}, bf16[512,384]{1,0:T(8,128)(2,1)}, bf16[512,384]{1,0:T(8,128)(2,1)}) custom-call(f32[3]{0:T(128)} %power_multiply_fusion.slopes_ref, bf16[512,192]{1,0:T(8,128)(2,1)} %fusion.8.q_ref, f32[1,512]{1,0:T(1,128)} %get-tuple-element.102.pq_ref, f32[2,512]{1,0:T(2,128)} %maximum_bitcast_fusion.pk_ref, ...), custom_call_target="tpu_custom_call" | custom-call | flops 8455716864 | bytes 524288 | tf_op jit(solution)/shard_map/attention_back/attend_back/pallas_call | solution.py:232
  225.6 1.8 collective-permute-done.14
  227.5 1.1 add_convert_fusion.2._
  228.6 1.5 collective-permute-start.16
  230.1 7.3 %attend_back.3 = (bf16[512,192]{1,0:T(8,128)(2,1)}, bf16[512,384]{1,0:T(8,128)(2,1)}, bf16[512,384]{1,0:T(8,128)(2,1)}) custom-call(f32[3]{0:T(128)} %power_multiply_fusion.slopes_ref, bf16[512,192]{1,0:T(8,128)(2,1)} %fusion.8.q_ref, f32[1,512]{1,0:T(1,128)} %get-tuple-element.102.pq_ref, f32[2,512]{1,0:T(2,128)} %maximum_bitcast_fusion.1.pk_ref, ...), custom_call_target="tpu_custom_call" | custom-call | flops 8455716864 | bytes 524288 | tf_op jit(solution)/shard_map/attention_back/attend_back/pallas_call | solution.py:232
  237.6 1.2 copy.100
  238.9 1.7 reshape.650
  240.7 1.3 add_convert_fusion.1
  244.8 0.9 constant_dynamic-slice_fusion.1
  245.8 1.2 collective-permute-done.22
  247.8 3.7 %all-to-all-start.8 = ((bf16[8,24,768]{2,1,0:T(8,128)(2,1)}), bf16[8,24,768]{2,1,0:T(8,128)(2,1)S(1)}, u32[]{:S(2)}, u32[]{:S(2)}) async-start(bf16[8,24,768]{2,1,0:T(8,128)(2,1)} %bitcast.223), calls=%async_computation.10 | async-start | bytes 589824 | tf_op jit(solution)/shard_map/ff_weight_grads/all_to_all | solution.py:888
  251.5 3.0 convolution_convert_fusion.1
  254.5 13.6 %reduce-scatter.4.cloned.1.call-done = bf16[192,512]{1,0:T(8,128)(2,1)} async-done(((bf16[768,512]{1,0:T(8,128)(2,1)}), bf16[192,512]{1,0:T(8,128)(2,1)}) %reduce-scatter.4.cloned.1.call-update) | async-done | bytes 196624 | tf_op jit(solution)/shard_map/attn_weight_grad/reduce_scatter | solution.py:923
  268.1 1.6 constant_dynamic-slice_fusion.2
  270.4 3.9 %all-to-all-start.6 = ((bf16[8,64,768]{2,1,0:T(8,128)(2,1)}), bf16[8,64,768]{2,1,0:T(8,128)(2,1)S(1)}, u32[]{:S(2)}, u32[]{:S(2)}) async-start(bf16[8,64,768]{2,1,0:T(8,128)(2,1)} %bitcast.212), calls=%async_computation.6 | async-start | bytes 1572864 | tf_op jit(solution)/shard_map/input_grad/all_to_all | solution.py:977
  274.3 1.2 fusion.6
  275.6 1.0 maximum_select_fusion.7
  276.6 1.5 collective-permute-start.20
  278.8 3.5 %collective-permute-done.20 = bf16[2,2,24,512]{3,2,1,0:T(8,128)(2,1)S(1)} collective-permute-done((bf16[2,2,24,512]{3,2,1,0:T(8,128)(2,1)S(1)}, bf16[2,2,24,512]{3,2,1,0:T(8,128)(2,1)S(1)}, u32[]{:S(2)}, u32[]{:S(2)}) %collective-permute-start.20) | collective-permute-done | bytes 98336 | tf_op jit(solution)/shard_map/attn_weight_grad/ppermute | solution.py:582
  282.3 1.9 collective-permute-start.21
  284.2 4.3 %collective-permute-done.18 = bf16[8,32,576]{2,1,0:T(8,128)(2,1)S(1)} collective-permute-done((bf16[8,32,576]{2,1,0:T(8,128)(2,1)S(1)}, bf16[8,32,576]{2,1,0:T(8,128)(2,1)S(1)}, u32[]{:S(2)}, u32[]{:S(2)}) %collective-permute-start.18) | collective-permute-done | bytes 294944 | tf_op jit(solution)/shard_map/qkv_weight_grad/ppermute | solution.py:582
  289.4 5.7 %all-to-all-done.6 = bf16[8,64,768]{2,1,0:T(8,128)(2,1)S(1)} async-done(((bf16[8,64,768]{2,1,0:T(8,128)(2,1)}), bf16[8,64,768]{2,1,0:T(8,128)(2,1)S(1)}, u32[]{:S(2)}, u32[]{:S(2)}) %all-to-all-start.6) | async-done | bytes 786464 | tf_op jit(solution)/shard_map/input_grad/all_to_all | solution.py:977
  295.1 3.6 %all-to-all-start.7 = ((bf16[8,32,576]{2,1,0:T(8,128)(2,1)}), bf16[8,32,576]{2,1,0:T(8,128)(2,1)S(1)}, u32[]{:S(2)}, u32[]{:S(2)}) async-start(bf16[8,32,576]{2,1,0:T(8,128)(2,1)} %fusion.18), calls=%async_computation.7 | async-start | bytes 655360 | tf_op jit(solution)/shard_map/qkv_weight_grad/all_to_all | solution.py:997
  301.3 1.5 reshape.667
  303.7 5.5 %all-to-all-done.7 = bf16[8,32,576]{2,1,0:T(8,128)(2,1)S(1)} async-done(((bf16[8,32,576]{2,1,0:T(8,128)(2,1)}), bf16[8,32,576]{2,1,0:T(8,128)(2,1)S(1)}, u32[]{:S(2)}, u32[]{:S(2)}) %all-to-all-start.7) | async-done | bytes 294944 | tf_op jit(solution)/shard_map/qkv_weight_grad/all_to_all | solution.py:997
  (206 shorter events, 32.8 us)
Async XLA Ops:
  10.5 8.5 %copy-start.18 = (bf16[96,768]{1,0:T(8,128)(2,1)S(1)}, bf16[96,768]{1,0:T(8,128)(2,1)}, u32[]{:S(2)}) copy-start(bf16[96,768]{1,0:T(8,128)(2,1)} %param.25) | copy-start | bytes 442372
  10.9 8.6 %copy-start.16 = (bf16[2,64,768]{2,1,0:T(8,128)(2,1)S(1)}, bf16[2,64,768]{2,1,0:T(8,128)(2,1)}, u32[]{:S(2)}) copy-start(bf16[2,64,768]{2,1,0:T(8,128)(2,1)} %param.15) | copy-start | bytes 589828
  10.9 11.7 %copy-start.19 = (bf16[24,768]{1,0:T(8,128)(2,1)S(1)}, bf16[24,768]{1,0:T(8,128)(2,1)}, u32[]{:S(2)}) copy-start(bf16[24,768]{1,0:T(8,128)(2,1)} %param.19) | copy-start | bytes 110596
  11.7 10.9 %copy-start.15 = (bf16[24,6144]{1,0:T(8,128)(2,1)S(1)}, bf16[24,6144]{1,0:T(8,128)(2,1)}, u32[]{:S(2)}) copy-start(bf16[24,6144]{1,0:T(8,128)(2,1)} %param.23) | copy-start | bytes 884740
  11.7 20.9 %all-to-all-start = ((bf16[8,32,640]{2,1,0:T(8,128)(2,1)}), bf16[8,32,640]{2,1,0:T(8,128)(2,1)S(1)}, u32[]{:S(2)}, u32[]{:S(2)}) async-start(bf16[8,32,640]{2,1,0:T(8,128)(2,1)} %bitcast.15), calls=%async_computation | async-start | bytes 655360 | tf_op jit(solution)/shard_map/gather_qkv_weights/all_to_all | solution.py:695
  19.5 4.7 %collective-permute-start.8 = (bf16[96,384]{1,0:T(8,128)(2,1)S(1)}, bf16[96,384]{1,0:T(8,128)(2,1)S(1)}, u32[]{:S(2)}, u32[]{:S(2)}) collective-permute-start(bf16[96,384]{1,0:T(8,128)(2,1)S(1)} %bitcast.231), channel_id=1, source_target_pairs={{0,1},{1,0},{2,3},{3,2},{4,5},{5,4},{6,7},{7,6},{8,9},{9,8},{10,11... | collective-permute-start | bytes 221192 | tf_op jit(solution)/shard_map/gather_ff_weights/ppermute | solution.py:752
  19.6 14.1 %collective-permute-start = (bf16[64,768]{1,0:T(8,128)(2,1)S(1)}, bf16[64,768]{1,0:T(8,128)(2,1)S(1)}, u32[]{:S(2)}, u32[]{:S(2)}) collective-permute-start(bf16[64,768]{1,0:T(8,128)(2,1)S(1)} %get-tuple-element.93), channel_id=1, source_target_pairs={{0,16},{16,0},{1,17},{17,1},{2,18},{18,2},{3,19},{19,3},{4,20},{20... | collective-permute-start | bytes 294920 | tf_op jit(solution)/shard_map/gather_tokens/ppermute | solution.py:700
  33.8 7.5 %collective-permute-start.1 = (bf16[2,64,768]{2,1,0:T(8,128)(2,1)S(1)}, bf16[2,64,768]{2,1,0:T(8,128)(2,1)S(1)}, u32[]{:S(2)}, u32[]{:S(2)}) collective-permute-start(bf16[2,64,768]{2,1,0:T(8,128)(2,1)S(1)} %fusion.29), channel_id=1, source_target_pairs={{0,8},{8,0},{1,9},{9,1},{2,10},{10,2},{3,11},{11,3},{4,12},{12,4},... | collective-permute-start | bytes 589832 | tf_op jit(solution)/shard_map/gather_tokens/ppermute | solution.py:703
  35.2 18.8 %all-to-all-start.2 = ((bf16[8,24,1152]{2,1,0:T(8,128)(2,1)}), bf16[8,24,1152]{2,1,0:T(8,128)(2,1)S(1)}, u32[]{:S(2)}, u32[]{:S(2)}) async-start(bf16[8,24,1152]{2,1,0:T(8,128)(2,1)} %maximum_add_fusion.1), calls=%async_computation.2 | async-start | bytes 884736 | tf_op jit(solution)/shard_map/gather_ff_weights/all_to_all | solution.py:749
  38.7 70.9 %all-gather.2.cloned.1.call-start = ((), (), s32[]{:S(2)}) async-start(), calls=%async_computation.12 | async-start | bytes 2949120 | tf_op jit(solution)/shard_map/gather_ff_weights/all_gather | solution.py:757
  39.3 14.3 %collective-permute-start.3 = (bf16[8,32,640]{2,1,0:T(8,128)(2,1)S(1)}, bf16[8,32,640]{2,1,0:T(8,128)(2,1)S(1)}, u32[]{:S(2)}, u32[]{:S(2)}) collective-permute-start(bf16[8,32,640]{2,1,0:T(8,128)(2,1)S(1)} %all-to-all-done), channel_id=1, source_target_pairs={{0,2},{2,0},{1,3},{3,1},{4,6},{6,4},{5,7},{7,5},{8,10},{10,8},{9,1... | collective-permute-start | bytes 983048 | tf_op jit(solution)/shard_map/gather_qkv_weights/ppermute | solution.py:709
  42.1 12.9 %collective-permute-start.2 = (bf16[2,2,64,768]{3,2,0,1:T(8,128)(2,1)}, bf16[2,2,64,768]{3,2,0,1:T(8,128)(2,1)S(1)}, u32[]{:S(2)}, u32[]{:S(2)}) collective-permute-start(bf16[2,2,64,768]{3,2,0,1:T(8,128)(2,1)} %maximum_select_fusion.4), channel_id=1, source_target_pairs={{0,4},{4,0},{1,5},{5,1},{2,6},{6,2},{3,7},{7,3},{8,12},{12,8},{9,1... | collective-permute-start | bytes 1179656 | tf_op jit(solution)/shard_map/gather_tokens/ppermute | solution.py:704
  53.7 2.3 collective-permute-start.4
  57.8 6.3 %copy-start.5 = (bf16[2,1,2,2,2,2,24,576]{7,6,5,4,3,2,0,1:T(8,128)(2,1)}, bf16[2,1,2,2,2,2,24,576]{7,6,5,4,3,2,0,1:T(8,128)(2,1)S(1)}, u32[]{:S(2)}) copy-start(bf16[2,1,2,2,2,2,24,576]{7,6,5,4,3,2,0,1:T(8,128)(2,1)S(1)} %copy.91) | copy-start | bytes 2654212
  60.7 11.9 %collective-permute-start.7 = (bf16[512,384]{1,0:T(8,128)(2,1)}, bf16[512,384]{1,0:T(8,128)(2,1)}, u32[]{:S(2)}, u32[]{:S(2)}) collective-permute-start(bf16[512,384]{1,0:T(8,128)(2,1)} %fusion.7.refs_0_), channel_id=1, source_target_pairs={{0,1},{1,0},{2,3},{3,2},{4,5},{5,4},{6,7},{7,6},{8,9},{9,8},{10,11... | collective-permute-start | bytes 1179656 | tf_op jit(solution)/shard_map/gather_kv/ppermute | solution.py:784
  61.0 11.5 %collective-permute-start.5 = (bf16[512,384]{1,0:T(8,128)(2,1)}, bf16[512,384]{1,0:T(8,128)(2,1)}, u32[]{:S(2)}, u32[]{:S(2)}) collective-permute-start(bf16[512,384]{1,0:T(8,128)(2,1)} %fusion.7.refs_0_), channel_id=1, source_target_pairs={{0,2},{2,0},{1,3},{3,1},{4,6},{6,4},{5,7},{7,5},{8,10},{10,8},{9,1... | collective-permute-start | bytes 1179656 | tf_op jit(solution)/shard_map/gather_kv/ppermute | solution.py:781
  72.5 5.4 %collective-permute-start.6 = (bf16[512,384]{1,0:T(8,128)(2,1)}, bf16[512,384]{1,0:T(8,128)(2,1)S(1)}, u32[]{:S(2)}, u32[]{:S(2)}) collective-permute-start(bf16[512,384]{1,0:T(8,128)(2,1)} %collective-permute-done.5.refs_0_), channel_id=1, source_target_pairs={{0,1},{1,0},{2,3},{3,2},{4,5},{5,4},{6,7},{7,6},{8,9},{9,8},{10,11... | collective-permute-start | bytes 1179656 | tf_op jit(solution)/shard_map/gather_kv/ppermute | solution.py:786
  77.9 0.7 copy-start.21
  110.7 4.3 %copy-start.11 = (bf16[768,384]{1,0:T(8,128)(2,1)}, bf16[768,384]{1,0:T(8,128)(2,1)S(1)}, u32[]{:S(2)}) copy-start(bf16[768,384]{1,0:T(8,128)(2,1)S(1)} %slice.131.own_ref) | copy-start | bytes 1769476
  110.8 4.3 %collective-permute-start.9 = (bf16[768,384]{1,0:T(8,128)(2,1)S(1)}, bf16[768,384]{1,0:T(8,128)(2,1)}, u32[]{:S(2)}, u32[]{:S(2)}) collective-permute-start(bf16[768,384]{1,0:T(8,128)(2,1)S(1)} %slice.131.own_ref), channel_id=1, source_target_pairs={{0,1},{1,0},{2,3},{3,2},{4,5},{5,4},{6,7},{7,6},{8,9},{9,8},{10,11... | collective-permute-start | bytes 1769480 | tf_op jit(solution)/shard_map/first_norm/ppermute | solution.py:826
  119.2 1.4 copy-start.6
  119.2 14.7 %collective-permute-start.10 = (bf16[768,1536]{1,0:T(8,128)(2,1)}, bf16[768,1536]{1,0:T(8,128)(2,1)}, u32[]{:S(2)}, u32[]{:S(2)}) collective-permute-start(bf16[768,1536]{1,0:T(8,128)(2,1)} %hold.4), channel_id=1, source_target_pairs={{0,1},{1,0},{2,3},{3,2},{4,5},{5,4},{6,7},{7,6},{8,9},{9,8},{10,11... | collective-permute-start | bytes 7077896 | tf_op jit(solution)/shard_map/first_norm/ppermute | solution.py:836
  171.8 6.9 %copy-start.9 = (bf16[512,768]{1,0:T(8,128)(2,1)S(1)}, bf16[512,768]{1,0:T(8,128)(2,1)}, u32[]{:S(2)}) copy-start(bf16[512,768]{1,0:T(8,128)(2,1)} %all_gather.10.hidden_ref) | copy-start | bytes 2359300
  178.7 3.1 copy-start.22
  178.7 3.1 copy-start.23
  181.8 7.8 %collective-permute-start.11 = (bf16[768,768]{1,0:T(8,128)(2,1)}, bf16[768,768]{1,0:T(8,128)(2,1)}, u32[]{:S(2)}, u32[]{:S(2)}) collective-permute-start(bf16[768,768]{1,0:T(8,128)(2,1)} %convolution_convert_fusion), channel_id=1, source_target_pairs={{0,1},{1,0},{2,3},{3,2},{4,5},{5,4},{6,7},{7,6},{8,9},{9,8},{10,11... | collective-permute-start | bytes 3538952 | tf_op jit(solution)/shard_map/ff_weight_grads/ppermute | solution.py:582
  182.4 4.1 %collective-permute-start.12 = (bf16[768,384]{1,0:T(8,128)(2,1)S(1)}, bf16[768,384]{1,0:T(8,128)(2,1)}, u32[]{:S(2)}, u32[]{:S(2)}) collective-permute-start(bf16[768,384]{1,0:T(8,128)(2,1)S(1)} %convolution_convert_fusion.3), channel_id=1, source_target_pairs={{0,1},{1,0},{2,3},{3,2},{4,5},{5,4},{6,7},{7,6},{8,9},{9,8},{10,11... | collective-permute-start | bytes 1769480 | tf_op jit(solution)/shard_map/ff_weight_grads/ppermute | solution.py:582
  183.0 14.8 %all-to-all-start.4 = ((bf16[4,128,768]{2,1,0:T(8,128)(2,1)}), bf16[4,128,768]{2,1,0:T(8,128)(2,1)S(1)}, u32[]{:S(2)}, u32[]{:S(2)}) async-start(bf16[4,128,768]{2,1,0:T(8,128)(2,1)} %bitcast.56), calls=%async_computation.4 | async-start | bytes 1572864 | tf_op jit(solution)/shard_map/sum_hidden_grad/all_to_all | solution.py:590
  186.5 58.3 %reduce-scatter.8.cloned.1.call-start = ((), (), s32[]{:S(2)}) async-start(), calls=%async_computation.15 | async-start | bytes 737280 | tf_op jit(solution)/shard_map/ff_weight_grads/reduce_scatter | solution.py:875
  186.5 3.1 copy-start.24
  188.7 4.0 %copy-start.10 = (bf16[768,384]{1,0:T(8,128)(2,1)}, bf16[768,384]{1,0:T(8,128)(2,1)S(1)}, u32[]{:S(2)}) copy-start(bf16[768,384]{1,0:T(8,128)(2,1)S(1)} %fusion.1.__) | copy-start | bytes 1769476
  197.7 0.9 copy-start.7
  198.7 3.4 %copy-start = (bf16[128,768]{1,0:T(8,128)(2,1)S(1)}, bf16[128,768]{1,0:T(8,128)(2,1)}, u32[]{:S(2)}) copy-start(bf16[128,768]{1,0:T(8,128)(2,1)} %reshape.637.refs_1_.mixed_ref) | copy-start | bytes 589828
  202.1 6.5 %copy-start.17 = (bf16[2,128,384]{2,1,0:T(8,128)(2,1)S(1)}, bf16[2,128,384]{2,1,0:T(8,128)(2,1)}, u32[]{:S(2)}) copy-start(bf16[2,128,384]{2,1,0:T(8,128)(2,1)} %get-tuple-element.73) | copy-start | bytes 589828
  204.4 4.6 %copy-start.8 = (bf16[768,128]{1,0:T(8,128)(2,1)S(1)}, bf16[768,128]{1,0:T(8,128)(2,1)}, u32[]{:S(2)}) copy-start(bf16[768,128]{1,0:T(8,128)(2,1)} %get-tuple-element.74) | copy-start | bytes 589828
  204.4 5.2 %collective-permute-start.13 = (bf16[768,512]{1,0:T(8,128)(2,1)S(1)}, bf16[768,512]{1,0:T(8,128)(2,1)}, u32[]{:S(2)}, u32[]{:S(2)}) collective-permute-start(bf16[768,512]{1,0:T(8,128)(2,1)S(1)} %pad_maximum_fusion), channel_id=1, source_target_pairs={{0,1},{1,0},{2,3},{3,2},{4,5},{5,4},{6,7},{7,6},{8,9},{9,8},{10,11... | collective-permute-start | bytes 2359304 | tf_op jit(solution)/shard_map/attn_weight_grad/ppermute | solution.py:582
  204.5 14.0 %all-to-all-start.5 = ((bf16[8,64,192]{2,1,0:T(8,128)(2,1)}), bf16[8,64,192]{2,1,0:T(8,128)(2,1)}, u32[]{:S(2)}, u32[]{:S(2)}) async-start(bf16[8,64,192]{2,1,0:T(8,128)(2,1)} %get-tuple-element.70), calls=%async_computation.5 | async-start | bytes 524288 | tf_op jit(solution)/shard_map/send_out_grad/all_to_all | solution.py:910
  208.6 39.2 %reduce-scatter.6.cloned.1.call-start = ((), (), s32[]{:S(2)}) async-start(), calls=%async_computation.14 | async-start | bytes 1474560 | tf_op jit(solution)/shard_map/ff_weight_grads/reduce_scatter | solution.py:874
  209.3 58.8 %reduce-scatter.4.cloned.1.call-start = ((), (), s32[]{:S(2)}) async-start(), calls=%async_computation.13 | async-start | bytes 983040 | tf_op jit(solution)/shard_map/attn_weight_grad/reduce_scatter | solution.py:923
  225.5 1.9 collective-permute-start.14
  228.6 1.5 copy-start.13
  228.6 12.1 %collective-permute-start.16 = (bf16[512,384]{1,0:T(8,128)(2,1)S(1)}, bf16[512,384]{1,0:T(8,128)(2,1)}, u32[]{:S(2)}, u32[]{:S(2)}) collective-permute-start(bf16[512,384]{1,0:T(8,128)(2,1)S(1)} %add_convert_fusion.2._), channel_id=1, source_target_pairs={{0,2},{2,0},{1,3},{3,1},{4,6},{6,4},{5,7},{7,5},{8,10},{10,8},{9,1... | collective-permute-start | bytes 1179656 | tf_op jit(solution)/shard_map/sum_kv_grads/ppermute | solution.py:582
  237.4 3.3 %collective-permute-start.15 = (bf16[512,384]{1,0:T(8,128)(2,1)}, bf16[512,384]{1,0:T(8,128)(2,1)}, u32[]{:S(2)}, u32[]{:S(2)}) collective-permute-start(bf16[512,384]{1,0:T(8,128)(2,1)} %get-tuple-element.80), channel_id=1, source_target_pairs={{0,1},{1,0},{2,3},{3,2},{4,5},{5,4},{6,7},{7,6},{8,9},{9,8},{10,11... | collective-permute-start | bytes 1179656 | tf_op jit(solution)/shard_map/sum_kv_grads/ppermute | solution.py:582
  238.9 1.7 copy-start.20
  238.9 1.8 copy-start.14
  240.6 1.5 copy-start.4
  240.7 1.8 copy-start.1
  244.2 30.0 %collective-permute-start.17 = (bf16[2,8,32,576]{3,2,1,0:T(8,128)(2,1)}, bf16[2,8,32,576]{3,2,1,0:T(8,128)(2,1)}, u32[]{:S(2)}, u32[]{:S(2)}) collective-permute-start(bf16[2,8,32,576]{3,2,1,0:T(8,128)(2,1)} %fusion.16), channel_id=1, source_target_pairs={{0,1},{1,0},{2,3},{3,2},{4,5},{5,4},{6,7},{7,6},{8,9},{9,8},{10,11... | collective-permute-start | bytes 1769480 | tf_op jit(solution)/shard_map/qkv_weight_grad/ppermute | solution.py:582
  245.7 1.3 collective-permute-start.22
  247.8 21.9 %all-to-all-start.8 = ((bf16[8,24,768]{2,1,0:T(8,128)(2,1)}), bf16[8,24,768]{2,1,0:T(8,128)(2,1)S(1)}, u32[]{:S(2)}, u32[]{:S(2)}) async-start(bf16[8,24,768]{2,1,0:T(8,128)(2,1)} %bitcast.223), calls=%async_computation.10 | async-start | bytes 589824 | tf_op jit(solution)/shard_map/ff_weight_grads/all_to_all | solution.py:888
  269.7 5.9 %collective-permute-start.19 = (bf16[4,24,512]{2,1,0:T(8,128)(2,1)}, bf16[4,24,512]{2,1,0:T(8,128)(2,1)}, u32[]{:S(2)}, u32[]{:S(2)}) collective-permute-start(bf16[4,24,512]{2,1,0:T(8,128)(2,1)} %get-tuple-element.91), channel_id=1, source_target_pairs={{0,1},{1,0},{2,3},{3,2},{4,5},{5,4},{6,7},{7,6},{8,9},{9,8},{10,11... | collective-permute-start | bytes 294920 | tf_op jit(solution)/shard_map/attn_weight_grad/ppermute | solution.py:926
  269.7 0.7 copy-start.2
  270.4 24.7 %all-to-all-start.6 = ((bf16[8,64,768]{2,1,0:T(8,128)(2,1)}), bf16[8,64,768]{2,1,0:T(8,128)(2,1)S(1)}, u32[]{:S(2)}, u32[]{:S(2)}) async-start(bf16[8,64,768]{2,1,0:T(8,128)(2,1)} %bitcast.212), calls=%async_computation.6 | async-start | bytes 1572864 | tf_op jit(solution)/shard_map/input_grad/all_to_all | solution.py:977
  276.6 5.7 %collective-permute-start.20 = (bf16[2,2,24,512]{3,2,1,0:T(8,128)(2,1)S(1)}, bf16[2,2,24,512]{3,2,1,0:T(8,128)(2,1)S(1)}, u32[]{:S(2)}, u32[]{:S(2)}) collective-permute-start(bf16[2,2,24,512]{3,2,1,0:T(8,128)(2,1)S(1)} %dynamic-slice_bitcast_fusion), channel_id=1, source_target_pairs={{0,2},{2,0},{1,3},{3,1},{4,6},{6,4},{5,7},{7,5},{8,10},{10,8},{9,1... | collective-permute-start | bytes 294920 | tf_op jit(solution)/shard_map/attn_weight_grad/ppermute | solution.py:582
  278.1 10.4 %collective-permute-start.18 = (bf16[8,32,576]{2,1,0:T(8,128)(2,1)S(1)}, bf16[8,32,576]{2,1,0:T(8,128)(2,1)S(1)}, u32[]{:S(2)}, u32[]{:S(2)}) collective-permute-start(bf16[8,32,576]{2,1,0:T(8,128)(2,1)S(1)} %fusion.26), channel_id=1, source_target_pairs={{0,2},{2,0},{1,3},{3,1},{4,6},{6,4},{5,7},{7,5},{8,10},{10,8},{9,1... | collective-permute-start | bytes 884744 | tf_op jit(solution)/shard_map/qkv_weight_grad/ppermute | solution.py:582
  282.3 17.9 %copy-start.3 = (bf16[8,24,768]{2,1,0:T(8,128)(2,1)S(1)}, bf16[8,24,768]{2,1,0:T(8,128)(2,1)}, u32[]{:S(2)}) copy-start(bf16[8,24,768]{2,1,0:T(8,128)(2,1)} %copy-done.2) | copy-start | bytes 884740
  282.3 7.0 %collective-permute-start.21 = (bf16[2,24,512]{2,1,0:T(8,128)(2,1)S(1)}, bf16[2,24,512]{2,1,0:T(8,128)(2,1)S(1)}, u32[]{:S(2)}, u32[]{:S(2)}) collective-permute-start(bf16[2,24,512]{2,1,0:T(8,128)(2,1)S(1)} %fusion.35), channel_id=1, source_target_pairs={{0,4},{4,0},{1,5},{5,1},{2,6},{6,2},{3,7},{7,3},{8,12},{12,8},{9,1... | collective-permute-start | bytes 147464 | tf_op jit(solution)/shard_map/attn_weight_grad/ppermute | solution.py:582
  295.1 14.1 %all-to-all-start.7 = ((bf16[8,32,576]{2,1,0:T(8,128)(2,1)}), bf16[8,32,576]{2,1,0:T(8,128)(2,1)S(1)}, u32[]{:S(2)}, u32[]{:S(2)}) async-start(bf16[8,32,576]{2,1,0:T(8,128)(2,1)} %fusion.18), calls=%async_computation.7 | async-start | bytes 655360 | tf_op jit(solution)/shard_map/qkv_weight_grad/all_to_all | solution.py:997
  301.3 1.7 copy-start.12
Sparse Core Ops, SparseCore 0:
  55.0 54.5 all-gather.1
  192.9 21.2 reduce-scatter.7
  216.5 27.3 reduce-scatter.5
  246.0 21.9 reduce-scatter.3
